TPU v7x, 128 devices: a whole 4x4x4 slice. The times are simulated.
128 devices in a mesh: row: 8 (over y, core), col: 16 (over z, x).
Axes of the slice: x: 4, y: 4, z: 4, core: 2. Of those that a mesh axis runs over, the one named last changes fastest.
Arguments:
- weight: bfloat16 [8192, 26624], P('row', 'col'), may hold values from -6 to 6
- momentum: float32 [8192, 26624], P('row', 'col'), may hold values from -6 to 6
- gradient: bfloat16 [8192, 26624], P('row', 'col'), may hold values from -6 to 6
- right_factor: float32 [26624, 128], P('col'), may hold values from -6 to 6
Outputs:
- new_weight: bfloat16 [8192, 26624], P('row', 'col')
- new_momentum: float32 [8192, 26624], P('row', 'col')
- new_right: float32 [26624, 128], P('col')
All inputs are finite; a program needn't handle non-finite values.
Results may differ from a plain program's by a relative error of at most 0.001.
Values sent between devices are 32-bit elements; how exact they have to be, the bound alone decides.
A program may use at most 128 MiB of HBM per device.

v0:
```python
import jax
import jax.numpy as jnp
from jax import lax
from jax.sharding import PartitionSpec as P

ROWS = 8192
COLS = 26624
RANK = 128


def orthonormal(panel, gram):
    lower = jnp.linalg.cholesky(gram)
    return lax.linalg.triangular_solve(lower, panel, left_side=False, lower=True, transpose_a=True)


def shards(weight, momentum, gradient, right_factor):
    hi = lax.Precision.HIGHEST
    accum = momentum + gradient.astype(jnp.float32)
    local_panel = jnp.dot(accum, right_factor, precision=hi)
    panel = lax.psum(local_panel, "col")
    gram = lax.psum(jnp.dot(panel.T, panel, precision=hi), "row")
    ortho = orthonormal(panel, gram)
    local_right = lax.dot_general(accum, ortho, (((0,), (0,)), ((), ())), precision=hi)
    scale_cols = jnp.sqrt(jnp.float32(COLS))
    right = lax.psum(local_right, "row")
    squares = lax.psum(jnp.sum(right * right, axis=0), "col")
    new_right = right * (scale_cols / jnp.sqrt(squares + 1e-06))
    new_momentum = accum - 0.2 * jnp.dot(ortho, right.T, precision=hi)
    factor = 0.5 * jnp.sqrt(jnp.float32(ROWS) / jnp.float32(RANK))
    new_weight = (
        weight.astype(jnp.float32) - factor * jnp.dot(ortho, new_right.T, precision=hi)
    ).astype(jnp.bfloat16)
    return (new_weight, new_momentum, new_right)


def solution(mesh):
    placed = (P("row", "col"), P("row", "col"), P("row", "col"), P("col", None))
    return jax.shard_map(
        shards,
        mesh=mesh,
        in_specs=placed,
        out_specs=(P("row", "col"), P("row", "col"), P("col", None)),
        check_vma=False,
    )
```

profile of v0, /device:TPU:0, one launch (start us, length us, event | category | flops | bytes accessed | tf_op | source)
XLA Modules:
  0.0 337.2 jit_solution(10196262279814882223)
XLA Ops:
  7.2 0.0 all-reduce.4.cloned.1.call-start
  7.2 1.1 copy-done
  8.3 9.1 %fusion.1 = f32[1024,128]{1,0:T(8,128)} fusion(f32[1664,128]{1,0:T(8,128)S(1)} %copy-done, f32[1024,1664]{1,0:T(8,128)} %param.5, bf16[1024,1664]{1,0:T(8,128)(2,1)} %param.6), kind=kOutput, calls=%fused_computation.4 | convolution fusion | flops 2620653568 | bytes 11599872 | tf_op jit(solution)/shard_map/dot_general | solution.py:19
  17.5 0.0 all-reduce.6.cloned.1.call-start
  17.5 88.0 %all-reduce.4.cloned.1.call-done = f32[1024,128]{1,0:T(8,128)} async-done(((f32[1024,128]{1,0:T(8,128)}), f32[1024,128]{1,0:T(8,128)}) %all-reduce.4.cloned.1.call-update) | async-done | bytes 524304 | tf_op jit(solution)/shard_map/psum | solution.py:20
  105.5 2.8 fusion.6
  108.3 0.0 all-reduce.6.cloned.1.call-update
  108.4 0.0 all-reduce.8.cloned.1.call-start
  108.4 58.1 %all-reduce.6.cloned.1.call-done = f32[128,128]{0,1:T(8,128)} async-done(((f32[128,128]{0,1:T(8,128)}), f32[128,128]{0,1:T(8,128)}) %all-reduce.6.cloned.1.call-update) | async-done | bytes 65552 | tf_op jit(solution)/shard_map/psum | solution.py:21
  166.5 0.9 copy.8
  167.5 0.9 fusion.5
  168.3 11.7 %cholesky.16 = f32[128,128]{1,0:T(8,128)S(1)} custom-call(f32[128,128]{1,0:T(8,128)S(1)} %fusion.5), custom_call_target="Cholesky" | custom-call | tf_op jit(solution)/shard_map/jit(cholesky)/cholesky | solution.py:12
  180.1 0.6 compare_reduce_fusion
  180.7 0.7 fusion.2
  181.4 9.8 %custom-call.6 = f32[1,128,128]{1,2,0:T(8,128)S(1)} custom-call(f32[1,128,128]{2,1,0:T(8,128)S(1)} %fusion.2), custom_call_target="InvertDiagBlocksLowerTriangular" | custom-call | tf_op jit(solution)/shard_map/triangular_solve | solution.py:13
  191.2 1.6 fusion.3
  192.8 14.5 %fusion = f32[1664,128]{1,0:T(8,128)} fusion(f32[1024,128]{1,0:T(8,128)S(1)} %fusion.3, f32[1024,1664]{1,0:T(8,128)} %param.5, bf16[1024,1664]{1,0:T(8,128)(2,1)} %param.6), kind=kOutput, calls=%fused_computation.3 | convolution fusion | flops 2620653568 | bytes 11599872 | tf_op jit(solution)/shard_map/dot_general | solution.py:23
  207.3 0.0 all-reduce.8.cloned.1.call-update
  207.3 61.0 %all-reduce.8.cloned.1.call-done = f32[1664,128]{1,0:T(8,128)} async-done(((f32[1664,128]{1,0:T(8,128)}), f32[1664,128]{1,0:T(8,128)}) %all-reduce.8.cloned.1.call-update) | async-done | bytes 851984 | tf_op jit(solution)/shard_map/psum | solution.py:25
  268.3 1.5 multiply_reduce_fusion
  269.8 40.5 %psum.31 = f32[128]{0:T(128)S(1)} all-reduce(f32[128]{0:T(128)S(1)} %multiply_reduce_fusion), channel_id=1, replica_groups=mesh['row'=8,'col'=16] {'col'}, use_global_device_ids=true, to_apply=%region_6.7 | all-reduce | flops 128 | bytes 1024 | tf_op jit(solution)/shard_map/psum | solution.py:26
  310.3 1.4 broadcast_multiply_fusion
  311.7 9.0 %subtract_convert_fusion = bf16[1024,1664]{1,0:T(8,128)(2,1)} fusion(bf16[1024,1664]{1,0:T(8,128)(2,1)} %param.4, f32[1024,128]{1,0:T(8,128)S(1)} %fusion.3, f32[1664,128]{1,0:T(8,128)S(1)} %broadcast_multiply_fusion), kind=kOutput, calls=%fused_computation.1 | convolution fusion | flops 2624061440 | bytes 8192000 | tf_op jit(solution)/shard_map/dot_general | solution.py:31
  320.8 10.0 %multiply_subtract_fusion = f32[1024,1664]{1,0:T(8,128)} fusion(f32[1024,128]{1,0:T(8,128)S(1)} %fusion.3, f32[1664,128]{1,0:T(8,128)S(1)} %copy-done.2, f32[1024,1664]{1,0:T(8,128)} %param.5, bf16[1024,1664]{1,0:T(8,128)(2,1)S(1)} %copy-done.1), kind=kOutput, calls=%fused_computation | convolution fusion | flops 2624061440 | bytes 18415616 | tf_op jit(solution)/shard_map/dot_general | solution.py:28
  (10 shorter events, 0.1 us)
Async XLA Ops:
  7.2 1.2 copy-start
  7.2 98.3 %all-reduce.4.cloned.1.call-start = ((), (), s32[]{:S(2)}) async-start(), calls=%async_computation | async-start | bytes 1048576 | tf_op jit(solution)/shard_map/psum | solution.py:20
  17.5 149.0 %all-reduce.6.cloned.1.call-start = ((), (), s32[]{:S(2)}) async-start(), calls=%async_computation.1 | async-start | bytes 131072 | tf_op jit(solution)/shard_map/psum | solution.py:21
  108.4 159.9 %all-reduce.8.cloned.1.call-start = ((), (), s32[]{:S(2)}) async-start(), calls=%async_computation.2 | async-start | bytes 1703936 | tf_op jit(solution)/shard_map/psum | solution.py:25
  268.3 52.4 %copy-start.2 = (f32[1664,128]{1,0:T(8,128)S(1)}, f32[1664,128]{1,0:T(8,128)}, u32[]{:S(2)}) copy-start(f32[1664,128]{1,0:T(8,128)} %all-reduce.8.cloned.1.call-done) | copy-start | bytes 2555908
  310.3 10.4 %copy-start.1 = (bf16[1024,1664]{1,0:T(8,128)(2,1)S(1)}, bf16[1024,1664]{1,0:T(8,128)(2,1)}, u32[]{:S(2)}) copy-start(bf16[1024,1664]{1,0:T(8,128)(2,1)} %param.6) | copy-start | bytes 10223620
  311.7 19.0 %copy-start.3 = (f32[1664,128]{1,0:T(8,128)}, f32[1664,128]{1,0:T(8,128)S(1)}, u32[]{:S(2)}) copy-start(f32[1664,128]{1,0:T(8,128)S(1)} %broadcast_multiply_fusion) | copy-start | bytes 2555908
Sparse Core Ops, SparseCore 0:
  17.6 87.8 all-reduce.3
  108.5 57.9 all-reduce.5
  207.5 60.8 all-reduce.7
where the time goes:
time: 338 us; the launch traced here: 337 us
  waiting for transfers between devices  207 us (61%)
  matrix products  47.1 us (14%)
  blocking collectives  40.5 us (12%)
  other arithmetic  26.5 us (8%)
  between operations  13.8 us (4%)
    psum x1, waiting for transfers between devices, shards(): panel = lax.psum(local_panel, 'col')  88 us
    psum x1, waiting for transfers between devices, shards(): right = lax.psum(local_right, 'row')  61 us
    psum x1, waiting for transfers between devices, shards(): gram = lax.psum(jnp.dot(panel.T, panel, precision=hi), 'row')  58.1 us
    psum x1, blocking collectives, shards(): squares = lax.psum(jnp.sum(right * right, axis=0), 'col')  40.5 us
    dot_general x1, matrix products, shards(): lax.dot_general(accum, ortho, (((0,), (0,)), ((), ())), precision=hi)  14.5 us
    another operation x3, other arithmetic, orthonormal(): lower = jnp.linalg.cholesky(gram)  12.4 us
    another operation x2, other arithmetic, orthonormal(): lax.linalg.triangular_solve(lower, panel, left_side=False, lower=True, tr...  10.5 us
    dot_general x1, matrix products, shards(): new_momentum = accum - 0.2 * jnp.dot(ortho, right.T, precision=hi)  9.95 us
  transfers between devices with their start and end apart: 3, of which 3 were waited for; matrix products, arithmetic and copies ran while one was open for 0% of the time, Pallas kernels for 0%

commit v1 on v0

v1 whole, which is shorter than its diff:
```python
import functools

import jax
import jax.numpy as jnp
from jax import lax
from jax.experimental import pallas as pl
from jax.experimental.pallas import tpu as pltpu
from jax.sharding import PartitionSpec as P

ROWS = 8192
COLS = 26624
RANK = 128
HI = lax.Precision.HIGHEST
MESH = pl.DeviceIdType.MESH
F32 = jnp.float32
BF16 = jnp.bfloat16

ZS, XS, YS, CORES = 4, 4, 4, 2
COL_DEVS = ZS * XS
ROW_DEVS = YS * CORES
MY_ROWS = ROWS // ROW_DEVS
MY_COLS = COLS // COL_DEVS
OWN = MY_ROWS // COL_DEVS
GROUP = OWN * XS
GROUPS = MY_ROWS // GROUP
GRAM_OWN = RANK // ROW_DEVS
HALF = RANK // CORES
BLOCK = HALF // YS
SUB = BLOCK // 2
CHUNKS = ((0, 896), (896, 768))
NCH = len(CHUNKS)
PIVOTS = 16

CORE, UP_RELAY, UP_OWN, DOWN_RELAY, DOWN_OWN, UP_SUM, DOWN_SUM = range(7)
AG_UP, AG_DOWN, AG_UP_HALF, AG_DOWN_HALF, PAIR_OWN, PAIR_UP, PAIR_DOWN, PAIR_UP_HALF, PAIR_DOWN_HALF = range(7, 16)
KINDS = 16


def dot(a, b, precision=None):
    return jnp.dot(a, b, precision=precision, preferred_element_type=F32)


def iota(shape, dim):
    return lax.broadcasted_iota(jnp.int32, shape, dim)


def eliminate(rows, first):
    ri, ci = iota(rows.shape, 0), iota(rows.shape, 1)
    cols = [jnp.broadcast_to(rows[:, first + j : first + j + 1], rows.shape) for j in range(PIVOTS)]
    for k in range(PIVOTS):
        scale = lax.rsqrt(cols[k][k : k + 1, :])
        row = jnp.where(ci[:1] == first + k, scale, rows[k : k + 1, :] * scale)
        mult = jnp.where(ri > k, cols[k] * scale, 0.0)
        cleared = jnp.where((ci == first + k) & (ri > k), 0.0, rows)
        rows = jnp.where(ri == k, row, cleared - mult * row)
        for j in range(k + 1, PIVOTS):
            cols[j] = cols[j] - mult * (cols[j][k : k + 1, :] * scale)
    return jnp.where((ci > ri + first) & (ci < first + PIVOTS), 0.0, rows)


def cholesky_block(work, block):
    first = block * PIVOTS
    after = first + PIVOTS
    done = eliminate(work[first:after, :], first)
    work[first:after, :] = done
    if after < RANK:
        ci = iota(done.shape, 1)
        factor = jnp.where(ci >= after, done, 0.0).T
        rest = work[after:, :]
        cj = iota(rest.shape, 1)
        rest = jnp.where((cj >= first) & (cj < after), 0.0, rest)
        work[after:, :] = rest - dot(factor[after:, :], done, HI)


def main_kernel(
    mom, grad, rf, w,
    nm, wv, ortho, rt, sq,
    hi, lo, gbuf, rbuf, rcat, psend, prs, pan, pt, gram_part, gram_in, gram, sloc, cbuf, ys, yin, stf, sq_send, sq_in,
    load_sem, mom_sem, grad_sem,
    rs_send, rs_recv, ag_send, ag_recv, gs_send, gs_recv, ga_send, ga_recv, y_send, y_recv, q_send, q_recv,
):
    row = lax.axis_index("row")
    col = lax.axis_index("col")
    y, core = row // CORES, row % CORES
    z, x = col // XS, col % XS
    pair = (y * CORES + 1 - core, col)
    up = (((y + 1) % YS) * CORES + core, col)
    down = (((y + YS - 1) % YS) * CORES + core, col)

    rf_copy = pltpu.make_async_copy(rf, rbuf, load_sem.at[0])
    rf_copy.start()
    g0 = (x + z) % GROUPS

    def group_of(j):
        return (g0 + 1 + j) % GROUPS

    def load(j):
        rows = pl.ds(pl.multiple_of(group_of(j) * GROUP, GROUP), GROUP)
        return (
            pltpu.make_async_copy(mom.at[rows, :], nm.at[rows, :], mom_sem.at[j]),
            pltpu.make_async_copy(grad.at[rows, :], gbuf.at[rows, :], grad_sem.at[j]),
        )

    for j in range(GROUPS):
        for c in load(j):
            c.start()
    w_copy = pltpu.make_async_copy(w, wv, load_sem.at[1])
    w_copy.start()

    barrier = pltpu.get_barrier_semaphore()

    def greet_col(k, _):
        pl.semaphore_signal(barrier, inc=1, device_id=(row, (col + k) % COL_DEVS), device_id_type=MESH)
        return 0

    def greet_row(k, _):
        pl.semaphore_signal(barrier, inc=1, device_id=((row + k) % ROW_DEVS, col), device_id_type=MESH)
        return 0

    lax.fori_loop(1, COL_DEVS, greet_col, 0)
    lax.fori_loop(1, ROW_DEVS, greet_row, 0)

    rf_copy.wait()
    r = rbuf[...]
    rh = r.astype(BF16)
    rcat[:, :RANK] = rh
    rcat[:, RANK:] = (r - rh.astype(F32)).astype(BF16)
    pl.semaphore_wait(barrier, COL_DEVS - 1 + ROW_DEVS - 1)

    def own_rows(c):
        cz, cx = c // XS, c % XS
        return pl.ds(pl.multiple_of((((cx + cz) % GROUPS) * XS + cx) * OWN, OWN), OWN)

    def rs_copy(to, slot):
        return pltpu.make_async_remote_copy(
            src_ref=psend.at[own_rows(to), :], dst_ref=prs.at[slot], send_sem=rs_send.at[to], recv_sem=rs_recv.at[slot],
            device_id=(row, to), device_id_type=MESH)

    def panel_group(j, _):
        for c in load(j):
            c.wait()
        g = group_of(j)
        base = pl.multiple_of(g * GROUP, GROUP)

        def split(i, _):
            rows = pl.ds(pl.multiple_of(base + i * 32, 32), 32)
            a = nm[rows, :] + gbuf[rows, :].astype(F32)
            nm[rows, :] = a
            h = a.astype(BF16)
            hi[rows, :] = h
            lo[rows, :] = (a - h.astype(F32)).astype(BF16)
            return 0

        lax.fori_loop(0, GROUP // 32, split, 0)
        rows = pl.ds(base, GROUP)
        p = dot(hi[rows, :], rcat[...])
        psend[rows, :] = p[:, :RANK] + p[:, RANK:] + dot(lo[rows, :], rcat[:, :RANK])
        for t in range(XS):
            to = ((g + GROUPS - t) % GROUPS) * XS + t

            @pl.when(to != col)
            def _():
                rs_copy(to, col).start()

        return 0

    lax.fori_loop(0, GROUPS, panel_group, 0)

    mine = own_rows(col)

    def rs_sum(k, acc):
        src = (col + k) % COL_DEVS
        rs_copy(src, src).wait_recv()
        return acc + prs[src]

    pan[mine, :] = lax.fori_loop(1, COL_DEVS, rs_sum, psend[mine, :])

    def ag_copy(to, owner):
        rows = own_rows(owner)
        return pltpu.make_async_remote_copy(
            src_ref=pan.at[rows, :], dst_ref=pan.at[rows, :], send_sem=ag_send.at[to], recv_sem=ag_recv.at[owner],
            device_id=(row, to), device_id_type=MESH)

    def ag_start(k, _):
        ag_copy((col + k) % COL_DEVS, col).start()
        return 0

    lax.fori_loop(1, COL_DEVS, ag_start, 0)

    def ag_wait(k, _):
        src = (col + k) % COL_DEVS
        ag_copy(src, src).wait_recv()
        return 0

    lax.fori_loop(1, COL_DEVS, ag_wait, 0)

    p = pan[...]
    p_t = p.T
    ph = p_t.astype(BF16)
    pt[:RANK, :] = ph
    pt[RANK:, :] = (p_t - ph.astype(F32)).astype(BF16)
    gram_part[...] = dot(p_t, p, HI)

    def gram_rows(c):
        return pl.ds(pl.multiple_of(c * GRAM_OWN, GRAM_OWN), GRAM_OWN)

    def gs_copy(to, slot):
        return pltpu.make_async_remote_copy(
            src_ref=gram_part.at[gram_rows(to), :], dst_ref=gram_in.at[slot], send_sem=gs_send.at[to], recv_sem=gs_recv.at[slot],
            device_id=(to, col), device_id_type=MESH)

    def gs_start(k, _):
        gs_copy((row + k) % ROW_DEVS, row).start()
        return 0

    lax.fori_loop(1, ROW_DEVS, gs_start, 0)

    def ycopy(kind, c, src, dst, to):
        return pltpu.make_async_remote_copy(
            src_ref=src, dst_ref=dst, send_sem=y_send.at[c, kind], recv_sem=y_recv.at[c, kind], device_id=to, device_id_type=MESH)

    def lanes(c):
        return pl.ds(CHUNKS[c][0], CHUNKS[c][1])

    def core_copy(c):
        theirs = pl.ds(pl.multiple_of((1 - core) * HALF, HALF), HALF)
        return ycopy(CORE, c, sloc.at[theirs, lanes(c)], cbuf.at[:, lanes(c)], pair)

    for c in range(NCH):
        t = dot(pt[...], hi[:, lanes(c)])
        sloc[:, lanes(c)] = t[:RANK] + t[RANK:] + dot(pt[:RANK, :], lo[:, lanes(c)])
        core_copy(c).start()

    def ga_copy(to, owner):
        return pltpu.make_async_remote_copy(
            src_ref=gram.at[gram_rows(owner), :], dst_ref=gram.at[gram_rows(owner), :], send_sem=ga_send.at[to], recv_sem=ga_recv.at[owner],
            device_id=(to, col), device_id_type=MESH)

    def gs_sum(k, acc):
        src = (row + k) % ROW_DEVS
        gs_copy(src, src).wait_recv()
        return acc + gram_in[src]

    gram[gram_rows(row), :] = lax.fori_loop(1, ROW_DEVS, gs_sum, gram_part[gram_rows(row), :])

    def ga_start(k, _):
        ga_copy((row + k) % ROW_DEVS, row).start()
        return 0

    lax.fori_loop(1, ROW_DEVS, ga_start, 0)

    def block(ref, b, half, c):
        start = pl.multiple_of((b % YS) * BLOCK + half * SUB, SUB)
        return ref.at[pl.ds(start, SUB), lanes(c)]

    TOP, BOTTOM = 0, 1

    def relay_copies(c):
        return (
            ycopy(UP_RELAY, c, block(ys, y + 2, TOP, c), yin.at[UP_RELAY, :, lanes(c)], up),
            ycopy(DOWN_RELAY, c, block(ys, y + 2, BOTTOM, c), yin.at[DOWN_RELAY, :, lanes(c)], down),
            ycopy(UP_OWN, c, block(ys, y + 1, BOTTOM, c), yin.at[UP_OWN, :, lanes(c)], up),
            ycopy(DOWN_OWN, c, block(ys, y + 3, TOP, c), yin.at[DOWN_OWN, :, lanes(c)], down),
        )

    def sum_copies(c):
        return (
            ycopy(UP_SUM, c, block(ys, y + 1, TOP, c), yin.at[UP_SUM, :, lanes(c)], up),
            ycopy(DOWN_SUM, c, block(ys, y + 3, BOTTOM, c), yin.at[DOWN_SUM, :, lanes(c)], down),
        )

    def scatter_1(c):
        core_copy(c).wait_recv()
        ours = pl.ds(pl.multiple_of(core * HALF, HALF), HALF)
        ys[:, lanes(c)] = sloc[ours, lanes(c)] + cbuf[:, lanes(c)]
        for cp in relay_copies(c):
            cp.start()

    def scatter_2(c):
        relays = relay_copies(c)
        sums = sum_copies(c)
        for relay, total, kind in ((relays[0], sums[0], UP_RELAY), (relays[1], sums[1], DOWN_RELAY)):
            relay.wait_recv()
            start = (y + 1) % YS * BLOCK if kind == UP_RELAY else (y + 3) % YS * BLOCK + SUB
            rows = pl.ds(pl.multiple_of(start, SUB), SUB)
            ys[rows, lanes(c)] = ys[rows, lanes(c)] + yin[kind, :, lanes(c)]
            total.start()

    def st_block(b, half, c):
        start = pl.multiple_of(core * HALF + (b % YS) * BLOCK + (half or 0) * SUB, SUB)
        return stf.at[pl.ds(start, BLOCK if half is None else SUB), lanes(c)]

    def gather_copies(c):
        own, above, below = st_block(y, None, c), st_block(y + 1, None, c), st_block(y + 3, None, c)
        far_top, far_bottom = st_block(y + 2, TOP, c), st_block(y + 2, BOTTOM, c)
        up_half, down_half = st_block(y + 3, TOP, c), st_block(y + 1, BOTTOM, c)
        return {
            AG_UP: ycopy(AG_UP, c, own, own, up),
            AG_DOWN: ycopy(AG_DOWN, c, own, own, down),
            PAIR_OWN: ycopy(PAIR_OWN, c, own, own, pair),
            AG_UP_HALF: ycopy(AG_UP_HALF, c, up_half, up_half, up),
            AG_DOWN_HALF: ycopy(AG_DOWN_HALF, c, down_half, down_half, down),
            PAIR_UP: ycopy(PAIR_UP, c, below, below, pair),
            PAIR_DOWN: ycopy(PAIR_DOWN, c, above, above, pair),
            PAIR_UP_HALF: ycopy(PAIR_UP_HALF, c, far_top, far_top, pair),
            PAIR_DOWN_HALF: ycopy(PAIR_DOWN_HALF, c, far_bottom, far_bottom, pair),
        }

    def gather_1(c):
        relays = relay_copies(c)
        sums = sum_copies(c)
        for cp in (relays[2], relays[3], sums[0], sums[1]):
            cp.wait_recv()
        top = pl.ds(pl.multiple_of(y * BLOCK, SUB), SUB)
        bottom = pl.ds(pl.multiple_of(y * BLOCK + SUB, SUB), SUB)
        at_top = pl.ds(pl.multiple_of(core * HALF + y * BLOCK, SUB), SUB)
        at_bottom = pl.ds(pl.multiple_of(core * HALF + y * BLOCK + SUB, SUB), SUB)
        stf[at_top, lanes(c)] = ys[top, lanes(c)] + yin[UP_SUM, :, lanes(c)] + yin[DOWN_OWN, :, lanes(c)]
        stf[at_bottom, lanes(c)] = ys[bottom, lanes(c)] + yin[DOWN_SUM, :, lanes(c)] + yin[UP_OWN, :, lanes(c)]
        cps = gather_copies(c)
        for kind in (AG_UP, AG_DOWN, PAIR_OWN):
            cps[kind].start()

    def gather_2(c):
        cps = gather_copies(c)
        for got, onward in ((AG_UP, (AG_UP_HALF, PAIR_UP)), (AG_DOWN, (AG_DOWN_HALF, PAIR_DOWN))):
            cps[got].wait_recv()
            for kind in onward:
                cps[kind].start()

    def gather_3(c):
        cps = gather_copies(c)
        for got, onward in ((AG_UP_HALF, PAIR_UP_HALF), (AG_DOWN_HALF, PAIR_DOWN_HALF)):
            cps[got].wait_recv()
            cps[onward].start()

    def gather_4(c):
        cps = gather_copies(c)
        for kind in (PAIR_OWN, PAIR_UP, PAIR_DOWN, PAIR_UP_HALF, PAIR_DOWN_HALF):
            cps[kind].wait_recv()

    scatter_1(0)
    scatter_1(1)

    def ga_wait(k, _):
        src = (row + k) % ROW_DEVS
        ga_copy(src, src).wait_recv()
        return 0

    lax.fori_loop(1, ROW_DEVS, ga_wait, 0)

    def ga_sent(k, _):
        ga_copy((row + k) % ROW_DEVS, row).wait_send()
        gs_copy((row + k) % ROW_DEVS, row).wait_send()
        return 0

    lax.fori_loop(1, ROW_DEVS, ga_sent, 0)

    steps = {
        0: lambda: scatter_2(0),
        1: lambda: scatter_2(1),
        2: lambda: gather_1(0),
        3: lambda: gather_1(1),
        4: lambda: gather_2(0),
        5: lambda: gather_2(1),
        6: lambda: gather_3(0),
        7: lambda: gather_3(1),
    }
    for b in range(RANK // PIVOTS):
        cholesky_block(gram, b)
        steps[b]()
    inverse = jnp.where(iota((RANK, RANK), 0) >= iota((RANK, RANK), 1), gram[...], 0.0)
    o = lax.dot_general(pan[...], inverse, (((1,), (1,)), ((), ())), precision=HI, preferred_element_type=F32)
    ortho[...] = o

    squares = jnp.zeros((RANK, RANK), F32)
    for c in range(NCH):
        gather_4(c)
        part = dot(inverse, stf[:, lanes(c)], HI)
        rt[:, lanes(c)] = part
        for i in range(CHUNKS[c][1] // RANK):
            tile = part[:, i * RANK : (i + 1) * RANK]
            squares += tile * tile
    sq_send[...] = jnp.broadcast_to(jnp.sum(squares.T, axis=0, keepdims=True), sq_send.shape)

    def q_copy(to, slot):
        return pltpu.make_async_remote_copy(
            src_ref=sq_send, dst_ref=sq_in.at[slot], send_sem=q_send.at[to], recv_sem=q_recv.at[slot],
            device_id=(row, to), device_id_type=MESH)

    def q_start(k, _):
        q_copy((col + k) % COL_DEVS, col).start()
        return 0

    lax.fori_loop(1, COL_DEVS, q_start, 0)

    def momentum(i, _):
        rows = pl.ds(pl.multiple_of(i * 128, 128), 128)
        nm[rows, :] = nm[rows, :] - 0.2 * dot(ortho[rows, :].astype(BF16), rt[...].astype(BF16))
        return 0

    lax.fori_loop(0, MY_ROWS // 128, momentum, 0)

    def q_sum(k, acc):
        src = (col + k) % COL_DEVS
        q_copy(src, src).wait_recv()
        return acc + sq_in[src]

    sq[...] = lax.fori_loop(1, COL_DEVS, q_sum, sq_send[...])

    w_copy.wait()

    def sent(k, _):
        to = (col + k) % COL_DEVS
        rs_copy(to, col).wait_send()
        ag_copy(to, col).wait_send()
        q_copy(to, col).wait_send()
        return 0

    lax.fori_loop(1, COL_DEVS, sent, 0)
    for c in range(NCH):
        for cp in (core_copy(c),) + relay_copies(c) + sum_copies(c) + tuple(gather_copies(c).values()):
            cp.wait_send()


def final_kernel(nm, wv, ortho, rt, sq, new_w, new_m, new_r, out, r_out, oc, rc, m_sem, w_sem, r_sem):
    steps = 8
    size = MY_ROWS // steps
    m_copy = pltpu.make_async_copy(nm, new_m, m_sem)
    m_copy.start()
    scale = jnp.sqrt(F32(COLS)) / jnp.sqrt(sq[:1, :] + 1e-06)
    factor = 0.5 * jnp.sqrt(F32(ROWS) / F32(RANK))
    rh = rt[...].astype(BF16)
    rc[:RANK, :] = rh
    rc[RANK:, :] = (rt[...] - rh.astype(F32)).astype(BF16)
    o = ortho[...] * (scale * factor)
    oh = o.astype(BF16)
    oc[:, :RANK] = oh
    oc[:, RANK:] = (o - oh.astype(F32)).astype(BF16)

    def w_copy(i):
        rows = pl.ds(pl.multiple_of(i * size, size), size)
        return pltpu.make_async_copy(out.at[rows, :], new_w.at[rows, :], w_sem.at[i])

    def weight(i, _):
        rows = pl.ds(pl.multiple_of(i * size, size), size)
        high = oc[rows, :RANK]
        step = dot(high, rc[:RANK, :]) + dot(high, rc[RANK:, :]) + dot(oc[rows, RANK:], rc[:RANK, :])
        out[rows, :] = (wv[rows, :].astype(F32) - step).astype(BF16)
        w_copy(i).start()
        return 0

    lax.fori_loop(0, steps, weight, 0)
    r_out[...] = rt[...].T * scale
    r_copy = pltpu.make_async_copy(r_out, new_r, r_sem)
    r_copy.start()

    def done(i, _):
        w_copy(i).wait()
        return 0

    lax.fori_loop(0, steps, done, 0)
    m_copy.wait()
    r_copy.wait()


def shards(weight, momentum, gradient, right_factor):
    hbm = pl.BlockSpec(memory_space=pltpu.HBM)
    vmem = pl.BlockSpec(memory_space=pltpu.VMEM)
    dma = pltpu.SemaphoreType.DMA
    held = pl.pallas_call(
        main_kernel,
        out_shape=(
            pltpu.VMEM((MY_ROWS, MY_COLS), F32),
            pltpu.VMEM((MY_ROWS, MY_COLS), BF16),
            pltpu.VMEM((MY_ROWS, RANK), F32),
            pltpu.VMEM((RANK, MY_COLS), F32),
            pltpu.VMEM((8, RANK), F32),
        ),
        in_specs=[hbm] * 4,
        out_specs=(vmem,) * 5,
        scratch_shapes=[
            pltpu.VMEM((MY_ROWS, MY_COLS), BF16),
            pltpu.VMEM((MY_ROWS, MY_COLS), BF16),
            pltpu.VMEM((MY_ROWS, MY_COLS), BF16),
            pltpu.VMEM((MY_COLS, RANK), F32),
            pltpu.VMEM((MY_COLS, 2 * RANK), BF16),
            pltpu.VMEM((MY_ROWS, RANK), F32),
            pltpu.VMEM((COL_DEVS, OWN, RANK), F32),
            pltpu.VMEM((MY_ROWS, RANK), F32),
            pltpu.VMEM((2 * RANK, MY_ROWS), BF16),
            pltpu.VMEM((RANK, RANK), F32),
            pltpu.VMEM((ROW_DEVS, GRAM_OWN, RANK), F32),
            pltpu.VMEM((RANK, RANK), F32),
            pltpu.VMEM((RANK, MY_COLS), F32),
            pltpu.VMEM((HALF, MY_COLS), F32),
            pltpu.VMEM((HALF, MY_COLS), F32),
            pltpu.VMEM((7, SUB, MY_COLS), F32),
            pltpu.VMEM((RANK, MY_COLS), F32),
            pltpu.VMEM((8, RANK), F32),
            pltpu.VMEM((COL_DEVS, 8, RANK), F32),
            dma((2,)), dma((GROUPS,)), dma((GROUPS,)),
            dma((COL_DEVS,)), dma((COL_DEVS,)), dma((COL_DEVS,)), dma((COL_DEVS,)),
            dma((ROW_DEVS,)), dma((ROW_DEVS,)), dma((ROW_DEVS,)), dma((ROW_DEVS,)),
            dma((NCH, KINDS)), dma((NCH, KINDS)),
            dma((COL_DEVS,)), dma((COL_DEVS,)),
        ],
        compiler_params=pltpu.CompilerParams(collective_id=0, has_side_effects=True, vmem_limit_bytes=40 << 20),
        name="dion_main",
    )(momentum, gradient, right_factor, weight)
    return pl.pallas_call(
        final_kernel,
        out_shape=(
            jax.ShapeDtypeStruct((MY_ROWS, MY_COLS), BF16),
            jax.ShapeDtypeStruct((MY_ROWS, MY_COLS), F32),
            jax.ShapeDtypeStruct((MY_COLS, RANK), F32),
        ),
        in_specs=[vmem] * 5,
        out_specs=(hbm,) * 3,
        scratch_shapes=[
            pltpu.VMEM((MY_ROWS, MY_COLS), BF16),
            pltpu.VMEM((MY_COLS, RANK), F32),
            pltpu.VMEM((MY_ROWS, 2 * RANK), BF16),
            pltpu.VMEM((2 * RANK, MY_COLS), BF16),
            dma, dma((8,)), dma,
        ],
        compiler_params=pltpu.CompilerParams(vmem_limit_bytes=24 << 20),
        name="dion_final",
    )(*held)


def solution(mesh):
    placed = (P("row", "col"), P("row", "col"), P("row", "col"), P("col", None))
    return jax.shard_map(
        shards,
        mesh=mesh,
        in_specs=placed,
        out_specs=(P("row", "col"), P("row", "col"), P("col", None)),
        check_vma=False,
    )
```

time: 338 us -> 63.1 us (0.19)
  waiting for transfers between devices: 207 us -> 0 us
  Pallas kernels: 0 us -> 61.2 us
  matrix products: 47.1 us -> 0 us
  blocking collectives: 40.5 us -> 0 us
  other arithmetic: 26.5 us -> 0 us
  between operations: 13.8 us -> 0.65 us
    psum x3 -> x0, waiting for transfers between devices: 207 us -> none  [the longest x1 88 us: shards(): panel = lax.psum(local_panel, 'col')]
    pallas_call x0 -> x2, Pallas kernels: none -> 61.2 us  [the longest x1 55.7 us: shards(): pl.pallas_call(main_kernel, out_shape=(pltpu.VMEM((MY_ROWS, MY_COLS), F32...]
    dot_general x5 -> x0, matrix products: 45.5 us -> none  [the longest x1 14.5 us: shards(): lax.dot_general(accum, ortho, (((0,), (0,)), ((), ())), precision=hi)]
    psum x1 -> x0, blocking collectives: 40.5 us -> none  [shards(): squares = lax.psum(jnp.sum(right * right, axis=0), 'col')]
    another operation x5 -> x0, other arithmetic: 22.9 us -> none  [the longest x3 12.4 us: orthonormal(): lower = jnp.linalg.cholesky(gram)]
  transfers between devices with their start and end apart: 3 -> 0, of which waited for: 3 -> 0; matrix products, arithmetic and copies ran while one was open for 0% -> 0% of each run, Pallas kernels for 0% -> 0%
where the time goes in v1:
time: 63.1 us; the launch traced here: 63 us
  Pallas kernels  61.2 us (97%)
  local copies, waits for them, and re-layouts  1.15 us (2%)
  between operations  0.65 us (1%)
    pallas_call x1, Pallas kernels, shards(): pl.pallas_call(main_kernel, out_shape=(pltpu.VMEM((MY_ROWS, MY_COLS), F32...  55.7 us
    pallas_call x1, Pallas kernels, shards(): pl.pallas_call(final_kernel, out_shape=(jax.ShapeDtypeStruct((MY_ROWS, MY...  5.45 us

profile of v1, /device:TPU:0, one launch (start us, length us, event | category | flops | bytes accessed | tf_op | source)
XLA Modules:
  0.0 63.0 jit_solution(16651472352071049935)
XLA Ops:
  0.6 0.0 copy-start
  0.6 1.1 %copy-done = f32[1664,128]{1,0:T(8,128)S(1)} copy-done((f32[1664,128]{1,0:T(8,128)S(1)}, f32[1664,128]{1,0:T(8,128)}, u32[]{:S(2)}) %copy-start) | copy-done | bytes 851992
  1.8 55.7 %dion_main.1 = (f32[1024,1664]{1,0:T(8,128)S(1)}, bf16[1024,1664]{1,0:T(8,128)(2,1)S(1)}, f32[1024,128]{1,0:T(8,128)S(1)}, f32[128,1664]{1,0:T(8,128)S(1)}, f32[8,128]{1,0:T(8,128)S(1)}) custom-call(f32[1024,1664]{1,0:T(8,128)} %mom.1, bf16[1024,1664]{1,0:T(8,128)(2,1)} %grad.1, f32[1664,128]{1,0:T(8,128)S(1)} %copy-done, bf16[1024,1664]{1,0:T(8,128)(2,1)} %w.1), custom_call_target="tpu_custom_call" | custom-call | tf_op jit(solution)/shard_map/dion_main/pallas_call | solution.py:471
  57.5 5.4 %dion_final.1 = (bf16[1024,1664]{1,0:T(8,128)(2,1)}, f32[1024,1664]{1,0:T(8,128)}, f32[1664,128]{1,0:T(8,128)}) custom-call(f32[1024,1664]{1,0:T(8,128)S(1)} %get-tuple-element.8.nm, bf16[1024,1664]{1,0:T(8,128)(2,1)S(1)} %get-tuple-element.9.wv, f32[1024,128]{1,0:T(8,128)S(1)} %get-tuple-element.10.ortho, f32[128,1664]{1,0:T(8,128)S(1)} %get-tuple-element.11.rt, ...), custom_call_target="tpu_custom_call" | custom-call | tf_op jit(solution)/shard_map/dion_final/pallas_call | solution.py:511
Async XLA Ops:
  0.6 1.2 %copy-start = (f32[1664,128]{1,0:T(8,128)S(1)}, f32[1664,128]{1,0:T(8,128)}, u32[]{:S(2)}) copy-start(f32[1664,128]{1,0:T(8,128)} %rf.1) | copy-start | bytes 2555908

commit v2 on v1

v2 whole, which is shorter than its diff:
```python
import jax
import jax.numpy as jnp
from jax import lax
from jax.experimental import pallas as pl
from jax.experimental.pallas import tpu as pltpu
from jax.sharding import PartitionSpec as P

ROWS = 8192
COLS = 26624
RANK = 128
HI = lax.Precision.HIGHEST
MESH = pl.DeviceIdType.MESH
F32 = jnp.float32
BF16 = jnp.bfloat16

ZS, XS, YS, CORES = 4, 4, 4, 2
COL_DEVS = ZS * XS
ROW_DEVS = YS * CORES
MY_ROWS = ROWS // ROW_DEVS
MY_COLS = COLS // COL_DEVS
OWN = MY_ROWS // COL_DEVS
GROUP = OWN * XS
GROUPS = MY_ROWS // GROUP
GRAM_OWN = RANK // ROW_DEVS
HALF = RANK // CORES
QUARTER = HALF // 2
CHUNKS = ((0, 512), (512, 512), (1024, 384), (1408, 256))
NCH = len(CHUNKS)
PIVOTS = 16

CORE, FIRST_A, FIRST_B, SECOND_A, SECOND_B, PAIR = range(6)
KINDS = 6


def dot(a, b, precision=None):
    return jnp.dot(a, b, precision=precision, preferred_element_type=F32)


def split(a):
    high = a.astype(BF16)
    return high, (a - high.astype(F32)).astype(BF16)


def dot3(a, b):
    ah, al = split(a)
    bh, bl = split(b)
    return dot(ah, bh) + (dot(ah, bl) + dot(al, bh))


def iota(shape, dim):
    return lax.broadcasted_iota(jnp.int32, shape, dim)


def eliminate(rows, first):
    ri, ci = iota(rows.shape, 0), iota(rows.shape, 1)
    cols = [jnp.broadcast_to(rows[:, first + j : first + j + 1], rows.shape) for j in range(PIVOTS)]
    for k in range(PIVOTS):
        scale = lax.rsqrt(cols[k][k : k + 1, :])
        row = jnp.where(ci[:1] == first + k, scale, rows[k : k + 1, :] * scale)
        mult = jnp.where(ri > k, cols[k] * scale, 0.0)
        cleared = jnp.where((ci == first + k) & (ri > k), 0.0, rows)
        rows = jnp.where(ri == k, row, cleared - mult * row)
        for j in range(k + 1, PIVOTS):
            cols[j] = cols[j] - mult * (cols[j][k : k + 1, :] * scale)
    return jnp.where((ci > ri + first) & (ci < first + PIVOTS), 0.0, rows)


def cholesky_block(work, block):
    first = block * PIVOTS
    after = first + PIVOTS
    done = eliminate(work[first:after, :], first)
    work[first:after, :] = done
    if after < RANK:
        ci = iota(done.shape, 1)
        factor = jnp.where(ci >= after, done, 0.0).T
        rest = work[after:, :]
        cj = iota(rest.shape, 1)
        rest = jnp.where((cj >= first) & (cj < after), 0.0, rest)
        work[after:, :] = rest - dot(factor[after:, :], done, HI)


def main_kernel(
    mom, grad, rf, w,
    nm, wv, ortho, rt, rcut, sq,
    hi, lo, gbuf, rbuf, rcat, psend, prs, pan, pt, gram_part, gram_in, gram, sloc, cbuf, y1, in1, y2, in2, stf, sq_send, sq_in,
    load_sem, mom_sem, grad_sem,
    rs_send, rs_recv, ag_send, ag_recv, gs_send, gs_recv, ga_send, ga_recv, y_send, y_recv, q_send, q_recv,
):
    row = lax.axis_index("row")
    col = lax.axis_index("col")
    y, core = row // CORES, row % CORES
    z, x = col // XS, col % XS
    pair = (y * CORES + 1 - core, col)
    near = ((y + 1 - 2 * (y % 2)) * CORES + core, col)
    far = ((YS - 1 - y) * CORES + core, col)

    rf_copy = pltpu.make_async_copy(rf, rbuf, load_sem.at[0])
    rf_copy.start()
    g0 = (x + z) % GROUPS

    def group_of(j):
        return (g0 + 1 + j) % GROUPS

    def load(j):
        rows = pl.ds(pl.multiple_of(group_of(j) * GROUP, GROUP), GROUP)
        return (
            pltpu.make_async_copy(mom.at[rows, :], nm.at[rows, :], mom_sem.at[j]),
            pltpu.make_async_copy(grad.at[rows, :], gbuf.at[rows, :], grad_sem.at[j]),
        )

    for j in range(GROUPS):
        for c in load(j):
            c.start()

    barrier = pltpu.get_barrier_semaphore()

    def greet_col(k, _):
        pl.semaphore_signal(barrier, inc=1, device_id=(row, (col + k) % COL_DEVS), device_id_type=MESH)
        return 0

    def greet_row(k, _):
        pl.semaphore_signal(barrier, inc=1, device_id=((row + k) % ROW_DEVS, col), device_id_type=MESH)
        return 0

    lax.fori_loop(1, COL_DEVS, greet_col, 0)
    lax.fori_loop(1, ROW_DEVS, greet_row, 0)

    rf_copy.wait()
    rh, rl = split(rbuf[...])
    rcat[:, :RANK] = rh
    rcat[:, RANK:] = rl

    def own_rows(c):
        cz, cx = c // XS, c % XS
        return pl.ds(pl.multiple_of((((cx + cz) % GROUPS) * XS + cx) * OWN, OWN), OWN)

    def rs_copy(to, slot):
        return pltpu.make_async_remote_copy(
            src_ref=psend.at[own_rows(to), :], dst_ref=prs.at[slot], send_sem=rs_send.at[to], recv_sem=rs_recv.at[slot],
            device_id=(row, to), device_id_type=MESH)

    def panel_group(j, _):
        for c in load(j):
            c.wait()
        g = group_of(j)
        rows = pl.ds(pl.multiple_of(g * GROUP, GROUP), GROUP)
        a = nm[rows, :] + gbuf[rows, :].astype(F32)
        nm[rows, :] = a
        ah, al = split(a)
        hi[rows, :] = ah
        lo[rows, :] = al
        p = dot(ah, rcat[...])
        psend[rows, :] = p[:, :RANK] + p[:, RANK:] + dot(al, rcat[:, :RANK])

        @pl.when(j == 0)
        def _():
            pl.semaphore_wait(barrier, COL_DEVS - 1 + ROW_DEVS - 1)

        for t in range(XS):
            to = ((g + GROUPS - t) % GROUPS) * XS + t

            @pl.when(to != col)
            def _():
                rs_copy(to, col).start()

        return 0

    lax.fori_loop(0, GROUPS, panel_group, 0)
    w_copy = pltpu.make_async_copy(w, wv, load_sem.at[1])
    w_copy.start()

    mine = own_rows(col)

    def rs_sum(k, acc):
        src = (col + k) % COL_DEVS
        rs_copy(src, src).wait_recv()
        return acc + prs[src]

    pan[mine, :] = lax.fori_loop(1, COL_DEVS, rs_sum, psend[mine, :])

    def ag_copy(to, owner):
        rows = own_rows(owner)
        return pltpu.make_async_remote_copy(
            src_ref=pan.at[rows, :], dst_ref=pan.at[rows, :], send_sem=ag_send.at[to], recv_sem=ag_recv.at[owner],
            device_id=(row, to), device_id_type=MESH)

    def ag_start(k, _):
        ag_copy((col + k) % COL_DEVS, col).start()
        return 0

    lax.fori_loop(1, COL_DEVS, ag_start, 0)

    def ag_wait(k, _):
        src = (col + k) % COL_DEVS
        ag_copy(src, src).wait_recv()
        return 0

    lax.fori_loop(1, COL_DEVS, ag_wait, 0)

    p = pan[...]
    p_t = p.T
    ph, p_low = split(p_t)
    pt[:RANK, :] = ph
    pt[RANK:, :] = p_low
    gram_part[...] = dot(p_t, p, HI)

    def gram_rows(c):
        return pl.ds(pl.multiple_of(c * GRAM_OWN, GRAM_OWN), GRAM_OWN)

    def gs_copy(to, slot):
        return pltpu.make_async_remote_copy(
            src_ref=gram_part.at[gram_rows(to), :], dst_ref=gram_in.at[slot], send_sem=gs_send.at[to], recv_sem=gs_recv.at[slot],
            device_id=(to, col), device_id_type=MESH)

    def gs_start(k, _):
        gs_copy((row + k) % ROW_DEVS, row).start()
        return 0

    lax.fori_loop(1, ROW_DEVS, gs_start, 0)

    def ycopy(kind, c, src, dst, to):
        return pltpu.make_async_remote_copy(
            src_ref=src, dst_ref=dst, send_sem=y_send.at[c, kind], recv_sem=y_recv.at[c, kind], device_id=to, device_id_type=MESH)

    def lanes(c):
        return pl.ds(CHUNKS[c][0], CHUNKS[c][1])

    def core_copy(c):
        theirs = pl.ds(pl.multiple_of((1 - core) * HALF, HALF), HALF)
        return ycopy(CORE, c, sloc.at[theirs, lanes(c)], cbuf.at[:, lanes(c)], pair)

    def quarter(ref, part, c):
        return ref.at[pl.ds(part * QUARTER, QUARTER), lanes(c)]

    def first_copies(c):
        return (
            ycopy(FIRST_A, c, quarter(y1, 0, c), quarter(in1, 0, c), near),
            ycopy(FIRST_B, c, quarter(y1, 1, c), quarter(in1, 1, c), far),
        )

    def second_copies(c):
        return (
            ycopy(SECOND_A, c, quarter(y2, 0, c), quarter(in2, 0, c), far),
            ycopy(SECOND_B, c, quarter(y2, 1, c), quarter(in2, 1, c), near),
        )

    ours = pl.ds(pl.multiple_of(core * HALF, HALF), HALF)

    def pair_copy(c):
        return ycopy(PAIR, c, stf.at[ours, lanes(c)], stf.at[ours, lanes(c)], pair)

    def first(c):
        core_copy(c).wait_recv()
        y1[:, lanes(c)] = sloc[ours, lanes(c)] + cbuf[:, lanes(c)]
        for cp in first_copies(c):
            cp.start()

    def second(c):
        for part, cp in enumerate(first_copies(c)):
            cp.wait_recv()
            at = pl.ds(part * QUARTER, QUARTER)
            y2[at, lanes(c)] = y1[at, lanes(c)] + in1[at, lanes(c)]
            second_copies(c)[part].start()

    def third(c):
        for cp in second_copies(c):
            cp.wait_recv()
        stf[ours, lanes(c)] = y2[:, lanes(c)] + in2[:, lanes(c)]
        pair_copy(c).start()

    for c in range(NCH):
        t = dot(pt[...], hi[:, lanes(c)])
        sloc[:, lanes(c)] = t[:RANK] + t[RANK:] + dot(pt[:RANK, :], lo[:, lanes(c)])
        core_copy(c).start()
        if c:
            first(c - 1)
    first(NCH - 1)

    def ga_copy(to, owner):
        return pltpu.make_async_remote_copy(
            src_ref=gram.at[gram_rows(owner), :], dst_ref=gram.at[gram_rows(owner), :], send_sem=ga_send.at[to], recv_sem=ga_recv.at[owner],
            device_id=(to, col), device_id_type=MESH)

    def gs_sum(k, acc):
        src = (row + k) % ROW_DEVS
        gs_copy(src, src).wait_recv()
        return acc + gram_in[src]

    gram[gram_rows(row), :] = lax.fori_loop(1, ROW_DEVS, gs_sum, gram_part[gram_rows(row), :])

    def ga_start(k, _):
        ga_copy((row + k) % ROW_DEVS, row).start()
        return 0

    lax.fori_loop(1, ROW_DEVS, ga_start, 0)

    for c in range(NCH):
        second(c)

    def ga_wait(k, _):
        src = (row + k) % ROW_DEVS
        ga_copy(src, src).wait_recv()
        return 0

    lax.fori_loop(1, ROW_DEVS, ga_wait, 0)

    def ga_sent(k, _):
        ga_copy((row + k) % ROW_DEVS, row).wait_send()
        gs_copy((row + k) % ROW_DEVS, row).wait_send()
        return 0

    lax.fori_loop(1, ROW_DEVS, ga_sent, 0)

    for b in range(RANK // PIVOTS):
        cholesky_block(gram, b)
        if b % 2 == 1:
            third(b // 2)
    inverse = jnp.where(iota((RANK, RANK), 0) >= iota((RANK, RANK), 1), gram[...], 0.0)
    ortho[...] = dot3(pan[...], inverse.T)

    squares = jnp.zeros((RANK, RANK), F32)
    for c in range(NCH):
        pair_copy(c).wait_recv()
        part = dot3(inverse, stf[:, lanes(c)])
        rt[:, lanes(c)] = part
        high, low = split(part)
        rcut[:RANK, lanes(c)] = high
        rcut[RANK : 2 * RANK, lanes(c)] = high
        rcut[2 * RANK :, lanes(c)] = low
        for i in range(CHUNKS[c][1] // RANK):
            tile = part[:, i * RANK : (i + 1) * RANK]
            squares += tile * tile
    sq_send[...] = jnp.broadcast_to(jnp.sum(squares.T, axis=0, keepdims=True), sq_send.shape)

    def q_copy(to, slot):
        return pltpu.make_async_remote_copy(
            src_ref=sq_send, dst_ref=sq_in.at[slot], send_sem=q_send.at[to], recv_sem=q_recv.at[slot],
            device_id=(row, to), device_id_type=MESH)

    def q_start(k, _):
        q_copy((col + k) % COL_DEVS, col).start()
        return 0

    lax.fori_loop(1, COL_DEVS, q_start, 0)

    def momentum(i, _):
        rows = pl.ds(pl.multiple_of(i * GROUP, GROUP), GROUP)
        nm[rows, :] = nm[rows, :] - 0.2 * dot(ortho[rows, :].astype(BF16), rcut[:RANK, :])
        return 0

    lax.fori_loop(0, GROUPS, momentum, 0)

    def q_sum(k, acc):
        src = (col + k) % COL_DEVS
        q_copy(src, src).wait_recv()
        return acc + sq_in[src]

    sq[...] = lax.fori_loop(1, COL_DEVS, q_sum, sq_send[...])

    w_copy.wait()

    def sent(k, _):
        to = (col + k) % COL_DEVS
        rs_copy(to, col).wait_send()
        ag_copy(to, col).wait_send()
        q_copy(to, col).wait_send()
        return 0

    lax.fori_loop(1, COL_DEVS, sent, 0)
    for c in range(NCH):
        for cp in (core_copy(c), pair_copy(c)) + first_copies(c) + second_copies(c):
            cp.wait_send()


def final_kernel(nm, wv, ortho, rt, rcut, sq, new_w, new_m, new_r, out, r_out, m_sem, w_sem, r_sem):
    m_copy = pltpu.make_async_copy(nm, new_m, m_sem)
    m_copy.start()
    scale = jnp.sqrt(F32(COLS)) / jnp.sqrt(sq[:1, :] + 1e-06)
    factor = 0.5 * jnp.sqrt(F32(ROWS) / F32(RANK))

    def w_copy(i):
        rows = pl.ds(pl.multiple_of(i * GROUP, GROUP), GROUP)
        return pltpu.make_async_copy(out.at[rows, :], new_w.at[rows, :], w_sem.at[i])

    def weight(i, _):
        rows = pl.ds(pl.multiple_of(i * GROUP, GROUP), GROUP)
        high, low = split(ortho[rows, :] * (scale * factor))
        step = dot(jnp.concatenate([high, low], axis=1), rcut[: 2 * RANK, :]) + dot(high, rcut[2 * RANK :, :])
        out[rows, :] = (wv[rows, :].astype(F32) - step).astype(BF16)
        w_copy(i).start()
        return 0

    lax.fori_loop(0, GROUPS, weight, 0)
    r_out[...] = rt[...].T * scale
    r_copy = pltpu.make_async_copy(r_out, new_r, r_sem)
    r_copy.start()

    def done(i, _):
        w_copy(i).wait()
        return 0

    lax.fori_loop(0, GROUPS, done, 0)
    m_copy.wait()
    r_copy.wait()


def shards(weight, momentum, gradient, right_factor):
    hbm = pl.BlockSpec(memory_space=pltpu.HBM)
    vmem = pl.BlockSpec(memory_space=pltpu.VMEM)
    dma = pltpu.SemaphoreType.DMA
    held = pl.pallas_call(
        main_kernel,
        out_shape=(
            pltpu.VMEM((MY_ROWS, MY_COLS), F32),
            pltpu.VMEM((MY_ROWS, MY_COLS), BF16),
            pltpu.VMEM((MY_ROWS, RANK), F32),
            pltpu.VMEM((RANK, MY_COLS), F32),
            pltpu.VMEM((3 * RANK, MY_COLS), BF16),
            pltpu.VMEM((8, RANK), F32),
        ),
        in_specs=[hbm] * 4,
        out_specs=(vmem,) * 6,
        scratch_shapes=[
            pltpu.VMEM((MY_ROWS, MY_COLS), BF16),
            pltpu.VMEM((MY_ROWS, MY_COLS), BF16),
            pltpu.VMEM((MY_ROWS, MY_COLS), BF16),
            pltpu.VMEM((MY_COLS, RANK), F32),
            pltpu.VMEM((MY_COLS, 2 * RANK), BF16),
            pltpu.VMEM((MY_ROWS, RANK), F32),
            pltpu.VMEM((COL_DEVS, OWN, RANK), F32),
            pltpu.VMEM((MY_ROWS, RANK), F32),
            pltpu.VMEM((2 * RANK, MY_ROWS), BF16),
            pltpu.VMEM((RANK, RANK), F32),
            pltpu.VMEM((ROW_DEVS, GRAM_OWN, RANK), F32),
            pltpu.VMEM((RANK, RANK), F32),
            pltpu.VMEM((RANK, MY_COLS), F32),
            pltpu.VMEM((HALF, MY_COLS), F32),
            pltpu.VMEM((HALF, MY_COLS), F32),
            pltpu.VMEM((HALF, MY_COLS), F32),
            pltpu.VMEM((HALF, MY_COLS), F32),
            pltpu.VMEM((HALF, MY_COLS), F32),
            pltpu.VMEM((RANK, MY_COLS), F32),
            pltpu.VMEM((8, RANK), F32),
            pltpu.VMEM((COL_DEVS, 8, RANK), F32),
            dma((2,)), dma((GROUPS,)), dma((GROUPS,)),
            dma((COL_DEVS,)), dma((COL_DEVS,)), dma((COL_DEVS,)), dma((COL_DEVS,)),
            dma((ROW_DEVS,)), dma((ROW_DEVS,)), dma((ROW_DEVS,)), dma((ROW_DEVS,)),
            dma((NCH, KINDS)), dma((NCH, KINDS)),
            dma((COL_DEVS,)), dma((COL_DEVS,)),
        ],
        compiler_params=pltpu.CompilerParams(collective_id=0, has_side_effects=True, vmem_limit_bytes=50 << 20),
        name="dion_main",
    )(momentum, gradient, right_factor, weight)
    return pl.pallas_call(
        final_kernel,
        out_shape=(
            jax.ShapeDtypeStruct((MY_ROWS, MY_COLS), BF16),
            jax.ShapeDtypeStruct((MY_ROWS, MY_COLS), F32),
            jax.ShapeDtypeStruct((MY_COLS, RANK), F32),
        ),
        in_specs=[vmem] * 6,
        out_specs=(hbm,) * 3,
        scratch_shapes=[
            pltpu.VMEM((MY_ROWS, MY_COLS), BF16),
            pltpu.VMEM((MY_COLS, RANK), F32),
            dma, dma((GROUPS,)), dma,
        ],
        compiler_params=pltpu.CompilerParams(vmem_limit_bytes=24 << 20),
        name="dion_final",
    )(*held)


def solution(mesh):
    placed = (P("row", "col"), P("row", "col"), P("row", "col"), P("col", None))
    return jax.shard_map(
        shards,
        mesh=mesh,
        in_specs=placed,
        out_specs=(P("row", "col"), P("row", "col"), P("col", None)),
        check_vma=False,
    )
```

time: 63.1 us -> 53.8 us (0.85)
  Pallas kernels: 61.2 us -> 52.5 us
  local copies, waits for them, and re-layouts: 1.15 us -> 0 us
    pallas_call x1, Pallas kernels: 55.7 us -> 48.3 us  [shards(): pl.pallas_call(main_kernel, out_shape=(pltpu.VMEM((MY_ROWS, MY_COLS), F32...]
    pallas_call x1, Pallas kernels: 5.45 us -> 4.22 us  [shards(): pl.pallas_call(final_kernel, out_shape=(jax.ShapeDtypeStruct((MY_ROWS, MY...]
    unnamed x2 -> x0, local copies, waits for them, and re-layouts: 1.15 us -> none
where the time goes in v2:
time: 53.8 us; the launch traced here: 53.1 us
  Pallas kernels  52.5 us (98%)
  between operations  0.64 us (1%)
    pallas_call x1, Pallas kernels, shards(): pl.pallas_call(main_kernel, out_shape=(pltpu.VMEM((MY_ROWS, MY_COLS), F32...  48.3 us
    pallas_call x1, Pallas kernels, shards(): pl.pallas_call(final_kernel, out_shape=(jax.ShapeDtypeStruct((MY_ROWS, MY...  4.22 us

profile of v2, /device:TPU:0, one launch (start us, length us, event | category | flops | bytes accessed | tf_op | source)
XLA Modules:
  0.0 53.1 jit_solution(13557063102091620764)
XLA Ops:
  0.6 48.3 %dion_main.1 = (f32[1024,1664]{1,0:T(8,128)S(1)}, bf16[1024,1664]{1,0:T(8,128)(2,1)S(1)}, f32[1024,128]{1,0:T(8,128)S(1)}, f32[128,1664]{1,0:T(8,128)S(1)}, bf16...) custom-call(f32[1024,1664]{1,0:T(8,128)} %mom.1, bf16[1024,1664]{1,0:T(8,128)(2,1)} %grad.1, f32[1664,128]{1,0:T(8,128)} %rf.1, ...), custom_call_target="tpu_custom_call" | custom-call | tf_op jit(solution)/shard_map/dion_main/pallas_call | solution.py:411
  48.9 4.2 %dion_final.1 = (bf16[1024,1664]{1,0:T(8,128)(2,1)}, f32[1024,1664]{1,0:T(8,128)}, f32[1664,128]{1,0:T(8,128)}) custom-call(f32[1024,1664]{1,0:T(8,128)S(1)} %get-tuple-element.9.nm, bf16[1024,1664]{1,0:T(8,128)(2,1)S(1)} %get-tuple-element.10.wv, f32[1024,128]{1,0:T(8,128)S(1)} %get-tuple-element.11.ortho, f32[128,1664]{1,0:T(8,128)S(1)} %get-tuple-element.12.rt, ...), custom_call_target="tpu_custom_call" | custom-call | tf_op jit(solution)/shard_map/dion_final/pallas_call | solution.py:454

commit v3 on v2

v3 whole, which is shorter than its diff:
```python
import jax
import jax.numpy as jnp
from jax import lax
from jax.experimental import pallas as pl
from jax.experimental.pallas import tpu as pltpu
from jax.sharding import PartitionSpec as P

ROWS = 8192
COLS = 26624
RANK = 128
HI = lax.Precision.HIGHEST
MESH = pl.DeviceIdType.MESH
F32 = jnp.float32
BF16 = jnp.bfloat16

ZS, XS, YS, CORES = 4, 4, 4, 2
COL_DEVS = ZS * XS
ROW_DEVS = YS * CORES
MY_ROWS = ROWS // ROW_DEVS
MY_COLS = COLS // COL_DEVS
OWN = MY_ROWS // COL_DEVS
GROUP = OWN * XS
GROUPS = MY_ROWS // GROUP
HALF = RANK // 2
SHARE = HALF // CORES
PART = SHARE // 2
PIECE = OWN // 2
SPAN = GROUP // 2
CHUNKS = ((0, 896), (896, 768))
NCH = len(CHUNKS)
UNITS = tuple((h, c) for h in range(2) for c in range(NCH))
PIVOTS = 16

CORE, FIRST_A, FIRST_B, SECOND_A, SECOND_B, PAIR = range(6)
KINDS = 6

FAR_FIRST = ((2, 2), (2, 1), (2, 3), (1, 2), (3, 2), (1, 1), (3, 3), (1, 3), (3, 1), (2, 0), (0, 2), (1, 0), (3, 0), (0, 1), (0, 3))


def dot(a, b, precision=None):
    return jnp.dot(a, b, precision=precision, preferred_element_type=F32)


def split(a):
    high = a.astype(BF16)
    return high, (a - high.astype(F32)).astype(BF16)


def dot3(a, b):
    ah, al = split(a)
    bh, bl = split(b)
    return dot(ah, bh) + (dot(ah, bl) + dot(al, bh))


def iota(shape, dim):
    return lax.broadcasted_iota(jnp.int32, shape, dim)


def eliminate(rows, first):
    ri, ci = iota(rows.shape, 0), iota(rows.shape, 1)
    cols = [jnp.broadcast_to(rows[:, first + j : first + j + 1], rows.shape) for j in range(PIVOTS)]
    for k in range(PIVOTS):
        scale = lax.rsqrt(cols[k][k : k + 1, :])
        row = jnp.where(ci[:1] == first + k, scale, rows[k : k + 1, :] * scale)
        mult = jnp.where(ri > k, cols[k] * scale, 0.0)
        cleared = jnp.where((ci == first + k) & (ri > k), 0.0, rows)
        rows = jnp.where(ri == k, row, cleared - mult * row)
        for j in range(k + 1, PIVOTS):
            cols[j] = cols[j] - mult * (cols[j][k : k + 1, :] * scale)
    return jnp.where((ci > ri + first) & (ci < first + PIVOTS), 0.0, rows)


def cholesky_block(work, block):
    first = block * PIVOTS
    after = first + PIVOTS
    done = eliminate(work[first:after, :], first)
    work[first:after, :] = done
    if after < RANK:
        ci = iota(done.shape, 1)
        factor = jnp.where(ci >= after, done, 0.0).T
        rest = work[after:, :]
        cj = iota(rest.shape, 1)
        rest = jnp.where((cj >= first) & (cj < after), 0.0, rest)
        work[after:, :] = rest - dot(factor[after:, :], done, HI)


def main_kernel(
    mom, grad, rf, w,
    nm, wv, ortho, rt, rcut, sq,
    hi, lo, gbuf, rbuf, rcat, psend, prs, pan, pan_t, pt, gram_part, gram_pair, gram_in, gram, sloc, cbuf, y1, in1, y2, in2, stf, sq_send, sq_in,
    load_sem, mom_sem, grad_sem,
    rs_send, rs_recv, ag_send, ag_recv, g_send, g_recv, y_send, y_recv, q_send, q_recv,
):
    row = lax.axis_index("row")
    col = lax.axis_index("col")
    y, core = row // CORES, row % CORES
    z, x = col // XS, col % XS
    pair = (y * CORES + 1 - core, col)
    near = ((y + 1 - 2 * (y % 2)) * CORES + core, col)
    far = ((YS - 1 - y) * CORES + core, col)

    barrier = pltpu.get_barrier_semaphore()

    def greet_col(k, _):
        pl.semaphore_signal(barrier, inc=1, device_id=(row, (col + k) % COL_DEVS), device_id_type=MESH)
        return 0

    lax.fori_loop(1, COL_DEVS, greet_col, 0)
    row_peers = [pair] + [(((y + k) % YS) * CORES + core, col) for k in (2, 1, 3)]
    for peer in row_peers:
        pl.semaphore_signal(barrier, inc=1, device_id=peer, device_id_type=MESH)

    rf_copy = pltpu.make_async_copy(rf, rbuf, load_sem.at[0])
    rf_copy.start()
    g0 = (x + z) % GROUPS

    def group_of(j):
        return (g0 + 1 + j) % GROUPS

    def other(step):
        return (z + step[0]) % ZS * XS + (x + step[1]) % XS

    def load(j):
        rows = pl.ds(pl.multiple_of(group_of(j) * GROUP, GROUP), GROUP)
        return (
            pltpu.make_async_copy(mom.at[rows, :], nm.at[rows, :], mom_sem.at[j]),
            pltpu.make_async_copy(grad.at[rows, :], gbuf.at[rows, :], grad_sem.at[j]),
        )

    for j in range(GROUPS):
        for c in load(j):
            c.start()

    rf_copy.wait()
    rh, rl = split(rbuf[...])
    rcat[:, :RANK] = rh
    rcat[:, RANK:] = rl

    def place(c):
        cz, cx = c // XS, c % XS
        return (cx + cz) % GROUPS * XS + cx

    def own_rows(c):
        return pl.ds(pl.multiple_of(place(c) * OWN, OWN), OWN)

    def rs_copy(to, slot):
        return pltpu.make_async_remote_copy(
            src_ref=psend.at[own_rows(to), :], dst_ref=prs.at[slot], send_sem=rs_send.at[to], recv_sem=rs_recv.at[slot],
            device_id=(row, to), device_id_type=MESH)

    def panel_group(j, _):
        for c in load(j):
            c.wait()
        g = group_of(j)
        rows = pl.ds(pl.multiple_of(g * GROUP, GROUP), GROUP)
        a = nm[rows, :] + gbuf[rows, :].astype(F32)
        nm[rows, :] = a
        ah, al = split(a)
        hi[rows, :] = ah
        lo[rows, :] = al
        p = dot(ah, rcat[...])
        p = p[:, :RANK] + p[:, RANK:] + dot(al, rcat[:, :RANK])
        for t in range(XS):
            at = pl.multiple_of(g * GROUP + t * OWN, OWN)
            psend[pl.ds(at, PIECE), :] = p[t * PIECE : (t + 1) * PIECE]
            psend[pl.ds(at + PIECE, PIECE), :] = p[SPAN + t * PIECE : SPAN + (t + 1) * PIECE]

        @pl.when(j == 0)
        def _():
            pl.semaphore_wait(barrier, COL_DEVS - 1 + len(row_peers))

        for t in range(XS):
            to = ((g + GROUPS - t) % GROUPS) * XS + t

            @pl.when(to != col)
            def _():
                rs_copy(to, col).start()

        return 0

    lax.fori_loop(0, GROUPS, panel_group, 0)
    w_copy = pltpu.make_async_copy(w, wv, load_sem.at[1])
    w_copy.start()

    mine = own_rows(col)

    total = psend[mine, :]
    for step in reversed(FAR_FIRST):
        src = other(step)
        rs_copy(src, src).wait_recv()
        total = total + prs[src]

    def own_block(c):
        return pl.ds(pl.multiple_of(place(c) * PIECE, PIECE), PIECE)

    for h in range(2):
        half = total[:, h * HALF : (h + 1) * HALF]
        pan[h, own_block(col), :] = jnp.concatenate([half[:PIECE], half[PIECE:]], axis=1)

    def ag_copy(h, to, owner):
        block = pan.at[h, own_block(owner), :]
        return pltpu.make_async_remote_copy(
            src_ref=block, dst_ref=block, send_sem=ag_send.at[h, to], recv_sem=ag_recv.at[h, owner],
            device_id=(row, to), device_id_type=MESH)

    for h in range(2):
        for step in FAR_FIRST:
            ag_copy(h, other(step), col).start()

    def arrive(h):
        def group(j, _):
            g = group_of(j)
            for t in range(XS):
                src = (g + GROUPS - t) % GROUPS * XS + t

                @pl.when(src != col)
                def _():
                    ag_copy(h, src, src).wait_recv()

            block = pan[h, pl.ds(pl.multiple_of(g * SPAN, SPAN), SPAN), :].T
            ranks = pl.ds(h * HALF, HALF)
            for i in range(2):
                at = pl.ds(pl.multiple_of(g * GROUP + i * SPAN, SPAN), SPAN)
                piece = block[i * HALF : (i + 1) * HALF]
                high, low = split(piece)
                pan_t[ranks, at] = piece
                pt[h, :HALF, at] = high
                pt[h, HALF:, at] = low
            if h == 1:
                both = pan_t[:, pl.ds(pl.multiple_of(g * GROUP, GROUP), GROUP)]
                gram_part[...] += lax.dot_general(both, both, (((1,), (1,)), ((), ())), precision=HI, preferred_element_type=F32)
            return 0

        lax.fori_loop(0, GROUPS, group, 0)

    gram_part[...] = jnp.zeros_like(gram_part)
    arrive(0)

    ours = pl.ds(pl.multiple_of(core * HALF, HALF), HALF)
    theirs = pl.ds(pl.multiple_of((1 - core) * HALF, HALF), HALF)

    def gram_copy(kind, src, dst, to):
        return pltpu.make_async_remote_copy(
            src_ref=src, dst_ref=dst, send_sem=g_send.at[kind], recv_sem=g_recv.at[kind], device_id=to, device_id_type=MESH)

    gram_scatter = gram_copy(0, gram_part.at[theirs, :], gram_pair, pair)
    gram_gather = gram_copy(1, gram.at[ours, :], gram.at[ours, :], pair)

    def gram_y(to, slot):
        return pltpu.make_async_remote_copy(
            src_ref=gram_in.at[slot], dst_ref=gram_in.at[slot], send_sem=g_send.at[2 + to], recv_sem=g_recv.at[2 + slot],
            device_id=(to * CORES + core, col), device_id_type=MESH)

    def gram_1():
        gram_scatter.wait_recv()
        gram_in[y] = gram_part[ours, :] + gram_pair[...]
        for k in (2, 1, 3):
            gram_y((y + k) % YS, y).start()

    def gram_2():
        for k in (1, 3, 2):
            src = (y + k) % YS
            gram_y(src, src).wait_recv()
        gram[ours, :] = (gram_in[0] + gram_in[1]) + (gram_in[2] + gram_in[3])
        gram_gather.start()

    def ycopy(kind, c, src, dst, to):
        return pltpu.make_async_remote_copy(
            src_ref=src, dst_ref=dst, send_sem=y_send.at[c, kind], recv_sem=y_recv.at[c, kind], device_id=to, device_id_type=MESH)

    def lanes(u):
        return pl.ds(*CHUNKS[UNITS[u][1]])

    def core_copy(u):
        return ycopy(CORE, u, sloc.at[ranks_of(u, 1 - core), lanes(u)], cbuf.at[share(u), lanes(u)], pair)

    def ranks_of(u, c):
        return pl.ds(pl.multiple_of(UNITS[u][0] * HALF + c * SHARE, SHARE), SHARE)

    def share(u):
        return pl.ds(UNITS[u][0] * SHARE, SHARE)

    def part_rows(u, part):
        return pl.ds(UNITS[u][0] * SHARE + part * PART, PART)

    def first_copies(u):
        return (
            ycopy(FIRST_A, u, y1.at[part_rows(u, 0), lanes(u)], in1.at[part_rows(u, 0), lanes(u)], near),
            ycopy(FIRST_B, u, y1.at[part_rows(u, 1), lanes(u)], in1.at[part_rows(u, 1), lanes(u)], far),
        )

    def second_copies(u):
        return (
            ycopy(SECOND_A, u, y2.at[part_rows(u, 0), lanes(u)], in2.at[part_rows(u, 0), lanes(u)], far),
            ycopy(SECOND_B, u, y2.at[part_rows(u, 1), lanes(u)], in2.at[part_rows(u, 1), lanes(u)], near),
        )

    def pair_copy(u):
        block = stf.at[ranks_of(u, core), lanes(u)]
        return ycopy(PAIR, u, block, block, pair)

    def product(u):
        h = UNITS[u][0]
        t = dot(pt[h], hi[:, lanes(u)])
        sloc[pl.ds(h * HALF, HALF), lanes(u)] = t[:HALF] + t[HALF:] + dot(pt[h, :HALF, :], lo[:, lanes(u)])
        core_copy(u).start()

    def first(u):
        core_copy(u).wait_recv()
        y1[share(u), lanes(u)] = sloc[ranks_of(u, core), lanes(u)] + cbuf[share(u), lanes(u)]
        for cp in first_copies(u):
            cp.start()

    def second(u):
        for part, cp in enumerate(first_copies(u)):
            cp.wait_recv()
            at = part_rows(u, part)
            y2[at, lanes(u)] = y1[at, lanes(u)] + in1[at, lanes(u)]
            second_copies(u)[part].start()

    def third(u):
        for cp in second_copies(u):
            cp.wait_recv()
        stf[ranks_of(u, core), lanes(u)] = y2[share(u), lanes(u)] + in2[share(u), lanes(u)]
        pair_copy(u).start()

    product(0)
    product(1)
    first(0)
    first(1)
    arrive(1)
    gram_scatter.start()
    product(2)
    product(3)
    gram_1()
    first(2)
    first(3)
    second(0)
    second(1)

    gram_2()
    second(2)
    gram_scatter.wait_send()
    gram_gather.wait()
    steps = {0: (second, 3), 2: (third, 0), 3: (third, 1), 5: (third, 2), 6: (third, 3)}
    for b in range(RANK // PIVOTS):
        cholesky_block(gram, b)
        if b in steps:
            move, u = steps[b]
            move(u)
    inverse = jnp.where(iota((RANK, RANK), 0) >= iota((RANK, RANK), 1), gram[...], 0.0)

    squares = jnp.zeros((RANK, RANK), F32)
    for c in range(NCH):
        pair_copy(c).wait_recv()
        pair_copy(NCH + c).wait_recv()
        part = dot3(inverse, stf[:, lanes(c)])
        rt[:, lanes(c)] = part
        for i in range(CHUNKS[c][1] // RANK):
            tile = part[:, i * RANK : (i + 1) * RANK]
            squares += tile * tile
    sq_send[...] = jnp.broadcast_to(jnp.sum(squares.T, axis=0, keepdims=True), sq_send.shape)

    def q_copy(to, slot):
        return pltpu.make_async_remote_copy(
            src_ref=sq_send, dst_ref=sq_in.at[slot], send_sem=q_send.at[to], recv_sem=q_recv.at[slot],
            device_id=(row, to), device_id_type=MESH)

    for step in FAR_FIRST:
        q_copy(other(step), col).start()

    ortho[...] = dot3(inverse, pan_t[...]).T
    high, low = split(rt[...])
    rcut[:RANK, :] = high
    rcut[RANK : 2 * RANK, :] = high
    rcut[2 * RANK :, :] = low

    def momentum(i, _):
        rows = pl.ds(pl.multiple_of(i * GROUP, GROUP), GROUP)
        nm[rows, :] = nm[rows, :] - 0.2 * dot(ortho[rows, :].astype(BF16), rcut[:RANK, :])
        return 0

    lax.fori_loop(0, GROUPS, momentum, 0)

    w_copy.wait()

    def sent(k, _):
        to = (col + k) % COL_DEVS
        rs_copy(to, col).wait_send()
        ag_copy(0, to, col).wait_send()
        ag_copy(1, to, col).wait_send()
        return 0

    lax.fori_loop(1, COL_DEVS, sent, 0)
    for k in (1, 2, 3):
        gram_y((y + k) % YS, y).wait_send()
    for u in range(len(UNITS)):
        for cp in (core_copy(u), pair_copy(u)) + first_copies(u) + second_copies(u):
            cp.wait_send()

    total = sq_send[...]
    for step in reversed(FAR_FIRST):
        src = other(step)
        q_copy(src, src).wait_recv()
        total = total + sq_in[src]
    sq[...] = total

    def q_sent(k, _):
        q_copy((col + k) % COL_DEVS, col).wait_send()
        return 0

    lax.fori_loop(1, COL_DEVS, q_sent, 0)


def final_kernel(nm, wv, ortho, rt, rcut, sq, new_w, new_m, new_r, out, r_out, m_sem, w_sem, r_sem):
    m_copy = pltpu.make_async_copy(nm, new_m, m_sem)
    m_copy.start()
    scale = jnp.sqrt(F32(COLS)) / jnp.sqrt(sq[:1, :] + 1e-06)
    factor = 0.5 * jnp.sqrt(F32(ROWS) / F32(RANK))

    def w_copy(i):
        rows = pl.ds(pl.multiple_of(i * GROUP, GROUP), GROUP)
        return pltpu.make_async_copy(out.at[rows, :], new_w.at[rows, :], w_sem.at[i])

    def weight(i, _):
        rows = pl.ds(pl.multiple_of(i * GROUP, GROUP), GROUP)
        high, low = split(ortho[rows, :] * (scale * factor))
        step = dot(jnp.concatenate([high, low], axis=1), rcut[: 2 * RANK, :]) + dot(high, rcut[2 * RANK :, :])
        out[rows, :] = (wv[rows, :].astype(F32) - step).astype(BF16)
        w_copy(i).start()
        return 0

    lax.fori_loop(0, GROUPS, weight, 0)
    r_out[...] = rt[...].T * scale
    r_copy = pltpu.make_async_copy(r_out, new_r, r_sem)
    r_copy.start()

    def done(i, _):
        w_copy(i).wait()
        return 0

    lax.fori_loop(0, GROUPS, done, 0)
    m_copy.wait()
    r_copy.wait()


def shards(weight, momentum, gradient, right_factor):
    hbm = pl.BlockSpec(memory_space=pltpu.HBM)
    vmem = pl.BlockSpec(memory_space=pltpu.VMEM)
    dma = pltpu.SemaphoreType.DMA
    held = pl.pallas_call(
        main_kernel,
        out_shape=(
            pltpu.VMEM((MY_ROWS, MY_COLS), F32),
            pltpu.VMEM((MY_ROWS, MY_COLS), BF16),
            pltpu.VMEM((MY_ROWS, RANK), F32),
            pltpu.VMEM((RANK, MY_COLS), F32),
            pltpu.VMEM((3 * RANK, MY_COLS), BF16),
            pltpu.VMEM((8, RANK), F32),
        ),
        in_specs=[hbm] * 4,
        out_specs=(vmem,) * 6,
        scratch_shapes=[
            pltpu.VMEM((MY_ROWS, MY_COLS), BF16),
            pltpu.VMEM((MY_ROWS, MY_COLS), BF16),
            pltpu.VMEM((MY_ROWS, MY_COLS), BF16),
            pltpu.VMEM((MY_COLS, RANK), F32),
            pltpu.VMEM((MY_COLS, 2 * RANK), BF16),
            pltpu.VMEM((MY_ROWS, RANK), F32),
            pltpu.VMEM((COL_DEVS, OWN, RANK), F32),
            pltpu.VMEM((2, MY_ROWS // 2, RANK), F32),
            pltpu.VMEM((RANK, MY_ROWS), F32),
            pltpu.VMEM((2, RANK, MY_ROWS), BF16),
            pltpu.VMEM((RANK, RANK), F32),
            pltpu.VMEM((HALF, RANK), F32),
            pltpu.VMEM((YS, HALF, RANK), F32),
            pltpu.VMEM((RANK, RANK), F32),
            pltpu.VMEM((RANK, MY_COLS), F32),
            pltpu.VMEM((HALF, MY_COLS), F32),
            pltpu.VMEM((HALF, MY_COLS), F32),
            pltpu.VMEM((HALF, MY_COLS), F32),
            pltpu.VMEM((HALF, MY_COLS), F32),
            pltpu.VMEM((HALF, MY_COLS), F32),
            pltpu.VMEM((RANK, MY_COLS), F32),
            pltpu.VMEM((8, RANK), F32),
            pltpu.VMEM((COL_DEVS, 8, RANK), F32),
            dma((2,)), dma((GROUPS,)), dma((GROUPS,)),
            dma((COL_DEVS,)), dma((COL_DEVS,)), dma((2, COL_DEVS)), dma((2, COL_DEVS)),
            dma((2 + YS,)), dma((2 + YS,)),
            dma((len(UNITS), KINDS)), dma((len(UNITS), KINDS)),
            dma((COL_DEVS,)), dma((COL_DEVS,)),
        ],
        compiler_params=pltpu.CompilerParams(collective_id=0, has_side_effects=True, vmem_limit_bytes=50 << 20),
        name="dion_main",
    )(momentum, gradient, right_factor, weight)
    return pl.pallas_call(
        final_kernel,
        out_shape=(
            jax.ShapeDtypeStruct((MY_ROWS, MY_COLS), BF16),
            jax.ShapeDtypeStruct((MY_ROWS, MY_COLS), F32),
            jax.ShapeDtypeStruct((MY_COLS, RANK), F32),
        ),
        in_specs=[vmem] * 6,
        out_specs=(hbm,) * 3,
        scratch_shapes=[
            pltpu.VMEM((MY_ROWS, MY_COLS), BF16),
            pltpu.VMEM((MY_COLS, RANK), F32),
            dma, dma((GROUPS,)), dma,
        ],
        compiler_params=pltpu.CompilerParams(vmem_limit_bytes=24 << 20),
        name="dion_final",
    )(*held)


def solution(mesh):
    placed = (P("row", "col"), P("row", "col"), P("row", "col"), P("col", None))
    return jax.shard_map(
        shards,
        mesh=mesh,
        in_specs=placed,
        out_specs=(P("row", "col"), P("row", "col"), P("col", None)),
        check_vma=False,
    )
```

time: 53.8 us -> 53.5 us (level)
  no operation moved by 1% of the time
where the time goes in v3:
time: 53.5 us; the launch traced here: 52.8 us
  Pallas kernels  52.1 us (97%)
  between operations  0.64 us (1%)
    pallas_call x1, Pallas kernels, shards(): pl.pallas_call(main_kernel, out_shape=(pltpu.VMEM((MY_ROWS, MY_COLS), F32...  47.9 us
    pallas_call x1, Pallas kernels, shards(): pl.pallas_call(final_kernel, out_shape=(jax.ShapeDtypeStruct((MY_ROWS, MY...  4.22 us

profile of v3, /device:TPU:0, one launch (start us, length us, event | category | flops | bytes accessed | tf_op | source)
XLA Modules:
  0.0 52.8 jit_solution(17211050639231914946)
XLA Ops:
  0.6 47.9 %dion_main.1 = (f32[1024,1664]{1,0:T(8,128)S(1)}, bf16[1024,1664]{1,0:T(8,128)(2,1)S(1)}, f32[1024,128]{1,0:T(8,128)S(1)}, f32[128,1664]{1,0:T(8,128)S(1)}, bf16...) custom-call(f32[1024,1664]{1,0:T(8,128)} %mom.1, bf16[1024,1664]{1,0:T(8,128)(2,1)} %grad.1, f32[1664,128]{1,0:T(8,128)} %rf.1, ...), custom_call_target="tpu_custom_call" | custom-call | tf_op jit(solution)/shard_map/dion_main/pallas_call | solution.py:451
  48.6 4.2 %dion_final.1 = (bf16[1024,1664]{1,0:T(8,128)(2,1)}, f32[1024,1664]{1,0:T(8,128)}, f32[1664,128]{1,0:T(8,128)}) custom-call(f32[1024,1664]{1,0:T(8,128)S(1)} %get-tuple-element.9.nm, bf16[1024,1664]{1,0:T(8,128)(2,1)S(1)} %get-tuple-element.10.wv, f32[1024,128]{1,0:T(8,128)S(1)} %get-tuple-element.11.ortho, f32[128,1664]{1,0:T(8,128)S(1)} %get-tuple-element.12.rt, ...), custom_call_target="tpu_custom_call" | custom-call | tf_op jit(solution)/shard_map/dion_final/pallas_call | solution.py:496

commit v4 on v3

--- a/solution.py
+++ b/solution.py
@@ -26,9 +26,8 @@
 PART = SHARE // 2
 PIECE = OWN // 2
 SPAN = GROUP // 2
-CHUNKS = ((0, 896), (896, 768))
-NCH = len(CHUNKS)
-UNITS = tuple((h, c) for h in range(2) for c in range(NCH))
+UNITS = ((0, 0, 896), (0, 896, 768), (1, 0, 512), (1, 512, 512), (1, 1024, 640))
+LATE = (2, 3, 4)
 PIVOTS = 16
 
 CORE, FIRST_A, FIRST_B, SECOND_A, SECOND_B, PAIR = range(6)
@@ -99,17 +98,6 @@
     near = ((y + 1 - 2 * (y % 2)) * CORES + core, col)
     far = ((YS - 1 - y) * CORES + core, col)
 
-    barrier = pltpu.get_barrier_semaphore()
-
-    def greet_col(k, _):
-        pl.semaphore_signal(barrier, inc=1, device_id=(row, (col + k) % COL_DEVS), device_id_type=MESH)
-        return 0
-
-    lax.fori_loop(1, COL_DEVS, greet_col, 0)
-    row_peers = [pair] + [(((y + k) % YS) * CORES + core, col) for k in (2, 1, 3)]
-    for peer in row_peers:
-        pl.semaphore_signal(barrier, inc=1, device_id=peer, device_id_type=MESH)
-
     rf_copy = pltpu.make_async_copy(rf, rbuf, load_sem.at[0])
     rf_copy.start()
     g0 = (x + z) % GROUPS
@@ -127,7 +115,21 @@
             pltpu.make_async_copy(grad.at[rows, :], gbuf.at[rows, :], grad_sem.at[j]),
         )
 
-    for j in range(GROUPS):
+    for c in load(0):
+        c.start()
+
+    barrier = pltpu.get_barrier_semaphore()
+
+    def greet_col(k, _):
+        pl.semaphore_signal(barrier, inc=1, device_id=(row, (col + k) % COL_DEVS), device_id_type=MESH)
+        return 0
+
+    lax.fori_loop(1, COL_DEVS, greet_col, 0)
+    row_peers = [pair] + [(((y + k) % YS) * CORES + core, col) for k in (2, 1, 3)]
+    for peer in row_peers:
+        pl.semaphore_signal(barrier, inc=1, device_id=peer, device_id_type=MESH)
+
+    for j in range(1, GROUPS):
         for c in load(j):
             c.start()
 
@@ -208,32 +210,19 @@
             ag_copy(h, other(step), col).start()
 
     def arrive(h):
-        def group(j, _):
-            g = group_of(j)
-            for t in range(XS):
-                src = (g + GROUPS - t) % GROUPS * XS + t
-
-                @pl.when(src != col)
-                def _():
-                    ag_copy(h, src, src).wait_recv()
-
-            block = pan[h, pl.ds(pl.multiple_of(g * SPAN, SPAN), SPAN), :].T
-            ranks = pl.ds(h * HALF, HALF)
+        for step in reversed(FAR_FIRST):
+            src = other(step)
+            ag_copy(h, src, src).wait_recv()
+        block = pan[h].T
+        for g in range(GROUPS):
             for i in range(2):
-                at = pl.ds(pl.multiple_of(g * GROUP + i * SPAN, SPAN), SPAN)
-                piece = block[i * HALF : (i + 1) * HALF]
+                at = pl.ds(g * GROUP + i * SPAN, SPAN)
+                piece = block[i * HALF : (i + 1) * HALF, g * SPAN : (g + 1) * SPAN]
                 high, low = split(piece)
-                pan_t[ranks, at] = piece
+                pan_t[h * HALF : (h + 1) * HALF, at] = piece
                 pt[h, :HALF, at] = high
                 pt[h, HALF:, at] = low
-            if h == 1:
-                both = pan_t[:, pl.ds(pl.multiple_of(g * GROUP, GROUP), GROUP)]
-                gram_part[...] += lax.dot_general(both, both, (((1,), (1,)), ((), ())), precision=HI, preferred_element_type=F32)
-            return 0
-
-        lax.fori_loop(0, GROUPS, group, 0)
-
-    gram_part[...] = jnp.zeros_like(gram_part)
+
     arrive(0)
 
     ours = pl.ds(pl.multiple_of(core * HALF, HALF), HALF)
@@ -269,7 +258,7 @@
             src_ref=src, dst_ref=dst, send_sem=y_send.at[c, kind], recv_sem=y_recv.at[c, kind], device_id=to, device_id_type=MESH)
 
     def lanes(u):
-        return pl.ds(*CHUNKS[UNITS[u][1]])
+        return pl.ds(*UNITS[u][1:])
 
     def core_copy(u):
         return ycopy(CORE, u, sloc.at[ranks_of(u, 1 - core), lanes(u)], cbuf.at[share(u), lanes(u)], pair)
@@ -329,20 +318,25 @@
     first(0)
     first(1)
     arrive(1)
+    gram_part[...] = lax.dot_general(pan_t[...], pan_t[...], (((1,), (1,)), ((), ())), precision=HI, preferred_element_type=F32)
     gram_scatter.start()
     product(2)
     product(3)
+    product(4)
     gram_1()
     first(2)
     first(3)
+    first(4)
     second(0)
     second(1)
+    second(2)
 
     gram_2()
-    second(2)
+    second(3)
+    second(4)
     gram_scatter.wait_send()
     gram_gather.wait()
-    steps = {0: (second, 3), 2: (third, 0), 3: (third, 1), 5: (third, 2), 6: (third, 3)}
+    steps = {2: (third, 0), 3: (third, 1), 4: (third, 2), 5: (third, 3), 6: (third, 4)}
     for b in range(RANK // PIVOTS):
         cholesky_block(gram, b)
         if b in steps:
@@ -351,12 +345,13 @@
     inverse = jnp.where(iota((RANK, RANK), 0) >= iota((RANK, RANK), 1), gram[...], 0.0)
 
     squares = jnp.zeros((RANK, RANK), F32)
-    for c in range(NCH):
-        pair_copy(c).wait_recv()
-        pair_copy(NCH + c).wait_recv()
-        part = dot3(inverse, stf[:, lanes(c)])
-        rt[:, lanes(c)] = part
-        for i in range(CHUNKS[c][1] // RANK):
+    for u in range(LATE[0]):
+        pair_copy(u).wait_recv()
+    for u in LATE:
+        pair_copy(u).wait_recv()
+        part = dot3(inverse, stf[:, lanes(u)])
+        rt[:, lanes(u)] = part
+        for i in range(UNITS[u][2] // RANK):
             tile = part[:, i * RANK : (i + 1) * RANK]
             squares += tile * tile
     sq_send[...] = jnp.broadcast_to(jnp.sum(squares.T, axis=0, keepdims=True), sq_send.shape)

time: 53.5 us -> 52.2 us (0.976)
  Pallas kernels: 52.1 us -> 50.9 us
    pallas_call x1, Pallas kernels: 47.9 us -> 46.7 us  [shards(): pl.pallas_call(main_kernel, out_shape=(pltpu.VMEM((MY_ROWS, MY_COLS), F32...]
where the time goes in v4:
time: 52.2 us; the launch traced here: 51.5 us
  Pallas kernels  50.9 us (98%)
  between operations  0.64 us (1%)
    pallas_call x1, Pallas kernels, shards(): pl.pallas_call(main_kernel, out_shape=(pltpu.VMEM((MY_ROWS, MY_COLS), F32...  46.7 us
    pallas_call x1, Pallas kernels, shards(): pl.pallas_call(final_kernel, out_shape=(jax.ShapeDtypeStruct((MY_ROWS, MY...  4.22 us

profile of v4, /device:TPU:0, one launch (start us, length us, event | category | flops | bytes accessed | tf_op | source)
XLA Modules:
  0.0 51.5 jit_solution(16897755244141377115)
XLA Ops:
  0.6 46.7 %dion_main.1 = (f32[1024,1664]{1,0:T(8,128)S(1)}, bf16[1024,1664]{1,0:T(8,128)(2,1)S(1)}, f32[1024,128]{1,0:T(8,128)S(1)}, f32[128,1664]{1,0:T(8,128)S(1)}, bf16...) custom-call(f32[1024,1664]{1,0:T(8,128)} %mom.1, bf16[1024,1664]{1,0:T(8,128)(2,1)} %grad.1, f32[1664,128]{1,0:T(8,128)} %rf.1, ...), custom_call_target="tpu_custom_call" | custom-call | tf_op jit(solution)/shard_map/dion_main/pallas_call | solution.py:446
  47.3 4.2 %dion_final.1 = (bf16[1024,1664]{1,0:T(8,128)(2,1)}, f32[1024,1664]{1,0:T(8,128)}, f32[1664,128]{1,0:T(8,128)}) custom-call(f32[1024,1664]{1,0:T(8,128)S(1)} %get-tuple-element.9.nm, bf16[1024,1664]{1,0:T(8,128)(2,1)S(1)} %get-tuple-element.10.wv, f32[1024,128]{1,0:T(8,128)S(1)} %get-tuple-element.11.ortho, f32[128,1664]{1,0:T(8,128)S(1)} %get-tuple-element.12.rt, ...), custom_call_target="tpu_custom_call" | custom-call | tf_op jit(solution)/shard_map/dion_final/pallas_call | solution.py:491

commit v5 on v4

--- a/solution.py
+++ b/solution.py
@@ -318,7 +318,9 @@
     first(0)
     first(1)
     arrive(1)
-    gram_part[...] = lax.dot_general(pan_t[...], pan_t[...], (((1,), (1,)), ((), ())), precision=HI, preferred_element_type=F32)
+    both = jnp.concatenate([pt[0, :HALF, :], pt[1, :HALF, :], pt[0, HALF:, :], pt[1, HALF:, :]], axis=0)
+    t = lax.dot_general(both, both, (((1,), (1,)), ((), ())), preferred_element_type=F32)
+    gram_part[...] = t[:RANK, :RANK] + (t[:RANK, RANK:] + t[RANK:, :RANK] + t[RANK:, RANK:])
     gram_scatter.start()
     product(2)
     product(3)
@@ -344,12 +346,15 @@
             move(u)
     inverse = jnp.where(iota((RANK, RANK), 0) >= iota((RANK, RANK), 1), gram[...], 0.0)
 
+    inverse_cut = jnp.concatenate(split(inverse), axis=0)
     squares = jnp.zeros((RANK, RANK), F32)
     for u in range(LATE[0]):
         pair_copy(u).wait_recv()
     for u in LATE:
         pair_copy(u).wait_recv()
-        part = dot3(inverse, stf[:, lanes(u)])
+        high, low = split(stf[:, lanes(u)])
+        t = dot(inverse_cut, high)
+        part = t[:RANK] + (t[RANK:] + dot(inverse_cut[:RANK], low))
         rt[:, lanes(u)] = part
         for i in range(UNITS[u][2] // RANK):
             tile = part[:, i * RANK : (i + 1) * RANK]

time: 52.2 us -> 51.8 us (level)
    pallas_call x1, Pallas kernels: 46.7 us -> 46.2 us  [shards(): pl.pallas_call(main_kernel, out_shape=(pltpu.VMEM((MY_ROWS, MY_COLS), F32...]
where the time goes in v5:
time: 51.8 us; the launch traced here: 51 us
  Pallas kernels  50.4 us (97%)
  between operations  0.64 us (1%)
    pallas_call x1, Pallas kernels, shards(): pl.pallas_call(main_kernel, out_shape=(pltpu.VMEM((MY_ROWS, MY_COLS), F32...  46.2 us
    pallas_call x1, Pallas kernels, shards(): pl.pallas_call(final_kernel, out_shape=(jax.ShapeDtypeStruct((MY_ROWS, MY...  4.22 us

profile of v5, /device:TPU:0, one launch (start us, length us, event | category | flops | bytes accessed | tf_op | source)
XLA Modules:
  0.0 51.0 jit_solution(12755932155836598721)
XLA Ops:
  0.6 46.2 %dion_main.1 = (f32[1024,1664]{1,0:T(8,128)S(1)}, bf16[1024,1664]{1,0:T(8,128)(2,1)S(1)}, f32[1024,128]{1,0:T(8,128)S(1)}, f32[128,1664]{1,0:T(8,128)S(1)}, bf16...) custom-call(f32[1024,1664]{1,0:T(8,128)} %mom.1, bf16[1024,1664]{1,0:T(8,128)(2,1)} %grad.1, f32[1664,128]{1,0:T(8,128)} %rf.1, ...), custom_call_target="tpu_custom_call" | custom-call | tf_op jit(solution)/shard_map/dion_main/pallas_call | solution.py:451
  46.8 4.2 %dion_final.1 = (bf16[1024,1664]{1,0:T(8,128)(2,1)}, f32[1024,1664]{1,0:T(8,128)}, f32[1664,128]{1,0:T(8,128)}) custom-call(f32[1024,1664]{1,0:T(8,128)S(1)} %get-tuple-element.9.nm, bf16[1024,1664]{1,0:T(8,128)(2,1)S(1)} %get-tuple-element.10.wv, f32[1024,128]{1,0:T(8,128)S(1)} %get-tuple-element.11.ortho, f32[128,1664]{1,0:T(8,128)S(1)} %get-tuple-element.12.rt, ...), custom_call_target="tpu_custom_call" | custom-call | tf_op jit(solution)/shard_map/dion_final/pallas_call | solution.py:496

commit v6 on v5

--- a/solution.py
+++ b/solution.py
@@ -195,10 +195,6 @@
     def own_block(c):
         return pl.ds(pl.multiple_of(place(c) * PIECE, PIECE), PIECE)
 
-    for h in range(2):
-        half = total[:, h * HALF : (h + 1) * HALF]
-        pan[h, own_block(col), :] = jnp.concatenate([half[:PIECE], half[PIECE:]], axis=1)
-
     def ag_copy(h, to, owner):
         block = pan.at[h, own_block(owner), :]
         return pltpu.make_async_remote_copy(
@@ -206,6 +202,8 @@
             device_id=(row, to), device_id_type=MESH)
 
     for h in range(2):
+        half = total[:, h * HALF : (h + 1) * HALF]
+        pan[h, own_block(col), :] = jnp.concatenate([half[:PIECE], half[PIECE:]], axis=1)
         for step in FAR_FIRST:
             ag_copy(h, other(step), col).start()
 

time: 51.8 us -> 51.8 us (level)
  no operation moved by 1% of the time
where the time goes in v6:
time: 51.8 us; the launch traced here: 51 us
  Pallas kernels  50.4 us (97%)
  between operations  0.64 us (1%)
    pallas_call x1, Pallas kernels, shards(): pl.pallas_call(main_kernel, out_shape=(pltpu.VMEM((MY_ROWS, MY_COLS), F32...  46.2 us
    pallas_call x1, Pallas kernels, shards(): pl.pallas_call(final_kernel, out_shape=(jax.ShapeDtypeStruct((MY_ROWS, MY...  4.22 us

profile of v6, /device:TPU:0, one launch (start us, length us, event | category | flops | bytes accessed | tf_op | source)
XLA Modules:
  0.0 51.0 jit_solution(8028233365059305938)
XLA Ops:
  0.6 46.2 %dion_main.1 = (f32[1024,1664]{1,0:T(8,128)S(1)}, bf16[1024,1664]{1,0:T(8,128)(2,1)S(1)}, f32[1024,128]{1,0:T(8,128)S(1)}, f32[128,1664]{1,0:T(8,128)S(1)}, bf16...) custom-call(f32[1024,1664]{1,0:T(8,128)} %mom.1, bf16[1024,1664]{1,0:T(8,128)(2,1)} %grad.1, f32[1664,128]{1,0:T(8,128)} %rf.1, ...), custom_call_target="tpu_custom_call" | custom-call | tf_op jit(solution)/shard_map/dion_main/pallas_call | solution.py:449
  46.8 4.2 %dion_final.1 = (bf16[1024,1664]{1,0:T(8,128)(2,1)}, f32[1024,1664]{1,0:T(8,128)}, f32[1664,128]{1,0:T(8,128)}) custom-call(f32[1024,1664]{1,0:T(8,128)S(1)} %get-tuple-element.9.nm, bf16[1024,1664]{1,0:T(8,128)(2,1)S(1)} %get-tuple-element.10.wv, f32[1024,128]{1,0:T(8,128)S(1)} %get-tuple-element.11.ortho, f32[128,1664]{1,0:T(8,128)S(1)} %get-tuple-element.12.rt, ...), custom_call_target="tpu_custom_call" | custom-call | tf_op jit(solution)/shard_map/dion_final/pallas_call | solution.py:494
